TPU v7x, 32 devices: a whole 2x2x4 slice. The times are simulated.
32 devices in a mesh: lat: 4 (over x, core), lon: 8 (over z, y).
Axes of the slice: x: 2, y: 2, z: 4, core: 2. Of those that a mesh axis runs over, the one named last changes fastest.
Arguments:
- control: float32 [80, 128, 1024], P(None, 'lat', 'lon'), may hold values from -6 to 6
- vertical: float32 [80, 80], replicated, may hold values from -0.625 to 0.625
- kappa: float32 [128, 1024], P('lat', 'lon'), may hold values from 0.03 to 0.24
- obs_weights: bfloat16 [80, 131072], P(None, ('lat', 'lon')), may hold values from -0.625 to 0.625
- obs_values: bfloat16 [131072], P(('lat', 'lon')), may hold values from -6 to 6
- obs_precision: bfloat16 [131072], P(('lat', 'lon')), may hold values from 0.5 to 4
- obs_slot: int32 [131072], P(('lat', 'lon')), may hold values from 0 to 8191, as said below
- obs_column: int32 [131072], P(('lat', 'lon')), may hold values from 0 to 4095
Outputs:
- gradient: float32 [80, 128, 1024], P(None, 'lat', 'lon')
Inputs may be any that keep to these rules, and one draw needn't show every extreme that they name: `obs_slot`: on each device the slots of its observations are distinct; slot // 256 is the owning device, numbered with the lat index slowest. At most 256 observations of one device go to one owner, and some owner receives exactly 256 from every device.
All inputs are finite; a program needn't handle non-finite values.
Results may differ from a plain program's by a relative error of at most 0.00035.
Values may be sent and summed in bfloat16 or wider, within the bound.
A program may use at most 64 MiB of HBM per device.

v0:
```python
import functools

import jax
import jax.numpy as jnp
from jax import lax
from jax.experimental import pallas as pl
from jax.experimental.pallas import tpu as pltpu
from jax.sharding import PartitionSpec as P

NSTEP = 4
LANES = 128
CHAINS = 8
VMEM = pl.BlockSpec(memory_space=pltpu.VMEM)
SMEM = pl.BlockSpec(memory_space=pltpu.SMEM)
PARAMS = pltpu.CompilerParams(vmem_limit_bytes=56 * 2**20)


def pack_kernel(slot_ref, payload_ref, out_ref, rows, slots):
    obs = rows.shape[0]

    @pl.loop(0, obs // LANES)
    def _(j):
        at = pl.multiple_of(j * LANES, LANES)
        rows[pl.ds(at, LANES), :] = payload_ref[:, pl.ds(at, LANES)].T

    @pl.loop(0, slots.shape[0] // 256)
    def _(j):
        at = pl.multiple_of(j * 256, 256)
        slots[pl.ds(at, 256), :] = jnp.zeros((256, LANES), jnp.float32)

    @pl.loop(0, obs // 32)
    def _(j):
        at = pl.multiple_of(j * 32, 32)
        for u in range(32):
            slots[pl.ds(slot_ref[at + u], 1), :] = rows[pl.ds(at + u, 1), :]

    @pl.loop(0, slots.shape[0] // 256)
    def _(j):
        at = pl.multiple_of(j * 256, 256)
        out_ref[pl.ds(at, 256), :] = slots[pl.ds(at, 256), :].astype(jnp.bfloat16)


def obs_kernel(levels, col_ref, got_ref, state_ref, out_ref, picked, *sums):
    count = picked.shape[0]
    cells = state_ref.shape[0]

    @pl.loop(0, cells // 256)
    def _(j):
        at = pl.multiple_of(j * 256, 256)
        for s in sums:
            s[pl.ds(at, 256), :] = jnp.zeros((256, LANES), jnp.float32)

    @pl.loop(0, count // 32)
    def _(j):
        at = pl.multiple_of(j * 32, 32)
        for u in range(32):
            picked[pl.ds(at + u, 1), :] = state_ref[pl.ds(col_ref[at + u], 1), :]

    @pl.loop(0, count // 128)
    def _(j):
        at = pl.multiple_of(j * 128, 128)
        w = got_ref[pl.ds(at, 128), :].astype(jnp.float32)
        model = jnp.sum(w * picked[pl.ds(at, 128), :], axis=1, keepdims=True)
        weighted = w[:, levels + 1 : levels + 2] * (model - w[:, levels : levels + 1])
        picked[pl.ds(at, 128), :] = w * weighted

    @pl.loop(0, count // 32)
    def _(j):
        at = pl.multiple_of(j * 32, 32)
        for u in range(0, 32, CHAINS):
            cols = [col_ref[at + u + c] for c in range(CHAINS)]
            old = [sums[c][pl.ds(cols[c], 1), :] for c in range(CHAINS)]
            for c in range(CHAINS):
                sums[c][pl.ds(cols[c], 1), :] = old[c] + picked[pl.ds(at + u + c, 1), :]

    @pl.loop(0, cells // 64)
    def _(j):
        at = pl.multiple_of(j * 64, 64)
        parts = [s[pl.ds(at, 64), :] for s in sums]
        while len(parts) > 1:
            parts = [a + b for a, b in zip(parts[::2], parts[1::2])]
        out_ref[pl.ds(at, 64), :] = parts[0]


def ring(row):
    width = row.shape[0]
    return pltpu.roll(row, 1, 0) + pltpu.roll(row, width - 1, 0)


def forward_kernel(field_ref, kappa_ref, out_ref, one, two):
    rows, lon = out_ref.shape[:2]
    total = field_ref.shape[0]
    source = field_ref
    for step in range(NSTEP):
        last = step == NSTEP - 1
        target = (one, two)[step % 2]

        @pl.loop(1 + step, total - 1 - step)
        def _(r):
            f = source[r]
            new = f + kappa_ref[r] * (source[r - 1] + source[r + 1] + ring(f) - 4.0 * f)
            if last:
                out_ref[r - NSTEP] = new[:lon]
            else:
                target[r] = new

        source = target


def adjoint_kernel(field_ref, kappa_ref, out_ref, z, y):
    rows, lon = out_ref.shape[:2]
    total = field_ref.shape[0]
    source = field_ref
    for step in range(NSTEP):
        last = step == NSTEP - 1

        @pl.loop(step, total - step)
        def _(r):
            y[r] = kappa_ref[r] * source[r]

        @pl.loop(1 + step, total - 1 - step)
        def _(r):
            f = y[r]
            new = source[r] + (y[r - 1] + y[r + 1] + ring(f) - 4.0 * f)
            if last:
                out_ref[r - NSTEP] = new[:lon]
            else:
                z[r] = new

        source = z


def exchange(block, axis, dim, periodic, dtype):
    count = lax.axis_size(axis)
    forward = [(i, i + 1) for i in range(count - 1)]
    if periodic:
        forward.append((count - 1, 0))
    backward = [(target, source) for source, target in forward]
    size = block.shape[dim]
    low = lax.slice_in_dim(block, size - NSTEP, None, axis=dim).astype(dtype)
    high = lax.slice_in_dim(block, 0, NSTEP, axis=dim).astype(dtype)
    low = lax.ppermute(low, axis, forward).astype(block.dtype)
    high = lax.ppermute(high, axis, backward).astype(block.dtype)
    return low, high


def extended(block, dtype):
    low, high = exchange(block, "lon", 1, True, dtype)
    block = jnp.concatenate([block, high, low], axis=1)
    low, high = exchange(block, "lat", 0, False, dtype)
    return jnp.concatenate([low, block, high], axis=0)


def local(control, vertical, kappa, obs_weights, obs_values, obs_precision, obs_slot, obs_column):
    levels, lat_rows, lon_cells = control.shape
    devices = lax.axis_size("lat") * lax.axis_size("lon")
    obs_here = obs_slot.shape[0]
    slot_count = 2 * obs_here // devices
    total = devices * slot_count
    cells = lat_rows * lon_cells
    f32 = jnp.float32

    payload = jnp.concatenate(
        [
            obs_weights.astype(f32),
            obs_values.astype(f32)[None],
            obs_precision.astype(f32)[None],
            (obs_column // lon_cells).astype(f32)[None],
            (obs_column % lon_cells).astype(f32)[None],
            jnp.zeros((LANES - levels - 4, obs_here), f32),
        ],
        axis=0,
    )
    send = pl.pallas_call(
        pack_kernel,
        out_shape=jax.ShapeDtypeStruct((total, LANES), jnp.bfloat16),
        in_specs=[SMEM, VMEM],
        out_specs=VMEM,
        scratch_shapes=[pltpu.VMEM((obs_here, LANES), f32), pltpu.VMEM((total, LANES), f32)],
        compiler_params=PARAMS,
        name="pack",
    )(obs_slot, payload)
    got = lax.all_to_all(
        send.reshape(devices, slot_count, LANES),
        ("lat", "lon"),
        split_axis=0,
        concat_axis=0,
        tiled=True,
    ).reshape(total, LANES)
    columns = (
        got[:, levels + 2].astype(f32) * lon_cells + got[:, levels + 3].astype(f32)
    ).astype(jnp.int32)

    kappa_ext = extended(kappa, f32)
    kappa_ext = jnp.broadcast_to(kappa_ext[:, :, None], kappa_ext.shape + (LANES,))
    wide = jnp.pad(vertical, ((0, LANES - levels), (0, 0)))
    start = jnp.einsum("kj,jab->abk", wide, control, precision=lax.Precision.HIGHEST)
    start = extended(start, f32)
    ext = start.shape
    state = pl.pallas_call(
        forward_kernel,
        out_shape=jax.ShapeDtypeStruct((lat_rows, lon_cells, LANES), f32),
        in_specs=[VMEM, VMEM],
        out_specs=VMEM,
        scratch_shapes=[pltpu.VMEM(ext, f32), pltpu.VMEM(ext, f32)],
        compiler_params=PARAMS,
        cost_estimate=pl.CostEstimate(flops=40 * start.size, bytes_accessed=12 * start.size, transcendentals=0),
        name="forward",
    )(start, kappa_ext)

    adjoint = pl.pallas_call(
        functools.partial(obs_kernel, levels),
        out_shape=jax.ShapeDtypeStruct((cells, LANES), f32),
        in_specs=[SMEM, VMEM, VMEM],
        out_specs=VMEM,
        scratch_shapes=[pltpu.VMEM((total, LANES), f32)] + [pltpu.VMEM((cells, LANES), f32)] * CHAINS,
        compiler_params=PARAMS,
        name="observe",
    )(columns, got, state.reshape(cells, LANES))

    adjoint = extended(adjoint.reshape(lat_rows, lon_cells, LANES), jnp.bfloat16)
    adjoint = pl.pallas_call(
        adjoint_kernel,
        out_shape=jax.ShapeDtypeStruct((lat_rows, lon_cells, LANES), f32),
        in_specs=[VMEM, VMEM],
        out_specs=VMEM,
        scratch_shapes=[pltpu.VMEM(ext, f32), pltpu.VMEM(ext, f32)],
        compiler_params=PARAMS,
        name="adjoint",
    )(adjoint, kappa_ext)
    back = jnp.einsum("jk,abj->kab", vertical, adjoint[:, :, :levels], precision=lax.Precision.HIGHEST)
    return control + back


def solution(mesh):
    in_specs = (
        P(None, "lat", "lon"),
        P(),
        P("lat", "lon"),
        P(None, ("lat", "lon")),
        P(("lat", "lon")),
        P(("lat", "lon")),
        P(("lat", "lon")),
        P(("lat", "lon")),
    )
    out_specs = P(None, "lat", "lon")
    return jax.shard_map(local, mesh=mesh, in_specs=in_specs, out_specs=out_specs, check_vma=False)
```

profile of v0, /device:TPU:1, one launch (start us, length us, event | category | flops | bytes accessed | tf_op | source)
XLA Modules:
  0.0 182.4 jit_solution(8166985161637713508)
XLA Ops:
  2.2 8.3 %concatenate.21.payload_ref = f32[128,4096]{1,0:T(8,128)} concatenate(bf16[80,4096]{1,0:T(8,128)(2,1)} %param.11, f32[1,4096]{1,0:T(1,128)S(1)} %bitcast.29, f32[1,4096]{1,0:T(1,128)S(1)} %bitcast.30, f32[1,4096]{1,0:T(1,128)S(1)} %bitcast.28, f32[1,4096]{1,0:T(1,128)S(1)} %bitcast.27, f32[44,4096]{1,0:T(8,128)S(1)} %broadcast_in_dim.33), dimensions={0} | concatenate | bytes 3538944 | tf_op jit(solution)/shard_map/concatenate | solution.py:163
  10.5 10.6 %pack.1 = bf16[8192,128]{1,0:T(8,128)(2,1)} custom-call(s32[4096]{0:T(1024)} %slot_ref.1, f32[128,4096]{1,0:T(8,128)} %concatenate.21.payload_ref), custom_call_target="tpu_custom_call" | custom-call | tf_op jit(solution)/shard_map/pack/pallas_call | solution.py:174
  21.1 7.1 %all-to-all-start = ((bf16[32,256,128]{2,1,0:T(8,128)(2,1)}), bf16[32,256,128]{2,1,0:T(8,128)(2,1)S(1)}, u32[]{:S(2)}, u32[]{:S(2)}) async-start(bf16[32,256,128]{2,1,0:T(8,128)(2,1)} %bitcast.25), calls=%async_computation | async-start | bytes 4194304 | tf_op jit(solution)/shard_map/all_to_all | solution.py:183
  28.3 3.7 %convolution_bitcast_fusion = f32[32,128,128]{2,1,0:T(8,128)S(1)} fusion(f32[80,32,128]{2,1,0:T(8,128)S(1)} %copy-done.2, f32[80,80]{0,1:T(8,128)S(1)} %copy.21), kind=kOutput, calls=%fused_computation.5 | convolution fusion | flops 503316480 | bytes 3433472 | tf_op jit(solution)/shard_map/kj,jab->abk/dot_general | solution.py:197
  32.1 4.2 %collective-permute-start = (f32[32,4,128]{2,1,0:T(4,128)S(1)}, f32[32,4,128]{2,1,0:T(4,128)S(1)}, u32[]{:S(2)}, u32[]{:S(2)}) collective-permute-start(f32[32,4,128]{2,1,0:T(4,128)S(1)} %get-tuple-element.9), channel_id=1, source_target_pairs={{1,0},{2,1},{3,2},{4,3},{5,4},{6,5},{7,6},{0,7},{9,8},{10,9},{11,1... | collective-permute-start | bytes 196616 | tf_op jit(solution)/shard_map/ppermute | solution.py:143
  36.4 27.8 %collective-permute-done = f32[32,4,128]{2,1,0:T(4,128)S(1)} collective-permute-done((f32[32,4,128]{2,1,0:T(4,128)S(1)}, f32[32,4,128]{2,1,0:T(4,128)S(1)}, u32[]{:S(2)}, u32[]{:S(2)}) %collective-permute-start) | collective-permute-done | bytes 65568 | tf_op jit(solution)/shard_map/ppermute | solution.py:143
  64.1 4.5 %collective-permute-done.1 = f32[32,4,128]{2,1,0:T(4,128)S(1)} collective-permute-done((f32[32,4,128]{2,1,0:T(4,128)S(1)}, f32[32,4,128]{2,1,0:T(4,128)S(1)}, u32[]{:S(2)}, u32[]{:S(2)}) %collective-permute-start.1) | collective-permute-done | bytes 65568 | tf_op jit(solution)/shard_map/ppermute | solution.py:142
  68.7 3.9 %collective-permute-start.2 = (f32[4,136,128]{2,1,0:T(8,128)S(1)}, f32[4,136,128]{2,1,0:T(8,128)S(1)}, u32[]{:S(2)}, u32[]{:S(2)}) collective-permute-start(f32[4,136,128]{2,1,0:T(8,128)S(1)} %get-tuple-element.7), channel_id=1, source_target_pairs={{0,8},{8,16},{16,24},{1,9},{9,17},{17,25},{2,10},{10,18},{18,26},{... | collective-permute-start | bytes 835592 | tf_op jit(solution)/shard_map/ppermute | solution.py:142
  72.6 1.9 %collective-permute-start.3 = (f32[4,136,128]{2,1,0:T(8,128)S(1)}, f32[4,136,128]{2,1,0:T(8,128)S(1)}, u32[]{:S(2)}, u32[]{:S(2)}) collective-permute-start(f32[4,136,128]{2,1,0:T(8,128)S(1)} %get-tuple-element.8), channel_id=1, source_target_pairs={{8,0},{16,8},{24,16},{9,1},{17,9},{25,17},{10,2},{18,10},{26,18},{... | collective-permute-start | bytes 835592 | tf_op jit(solution)/shard_map/ppermute | solution.py:143
  77.2 2.9 %collective-permute-done.5 = f32[32,4]{1,0:T(8,128)S(1)} collective-permute-done((f32[32,4]{1,0:T(8,128)S(1)}, f32[32,4]{1,0:T(8,128)S(1)}, u32[]{:S(2)}, u32[]{:S(2)}) %collective-permute-start.5) | collective-permute-done | bytes 544 | tf_op jit(solution)/shard_map/ppermute | solution.py:142
  80.1 5.1 %collective-permute-start.6 = (f32[4,136]{1,0:T(4,128)S(1)}, f32[4,136]{1,0:T(4,128)S(1)}, u32[]{:S(2)}, u32[]{:S(2)}) collective-permute-start(f32[4,136]{1,0:T(4,128)S(1)} %get-tuple-element.13), channel_id=1, source_target_pairs={{0,8},{8,16},{16,24},{1,9},{9,17},{17,25},{2,10},{10,18},{18,26},{... | collective-permute-start | bytes 6536 | tf_op jit(solution)/shard_map/ppermute | solution.py:142
  85.2 1.9 %collective-permute-start.7 = (f32[4,136]{1,0:T(4,128)S(1)}, f32[4,136]{1,0:T(4,128)S(1)}, u32[]{:S(2)}, u32[]{:S(2)}) collective-permute-start(f32[4,136]{1,0:T(4,128)S(1)} %get-tuple-element.14), channel_id=1, source_target_pairs={{8,0},{16,8},{24,16},{9,1},{17,9},{25,17},{10,2},{18,10},{26,18},{... | collective-permute-start | bytes 6536 | tf_op jit(solution)/shard_map/ppermute | solution.py:143
  87.1 3.0 %collective-permute-done.7 = f32[4,136]{1,0:T(4,128)S(1)} collective-permute-done((f32[4,136]{1,0:T(4,128)S(1)}, f32[4,136]{1,0:T(4,128)S(1)}, u32[]{:S(2)}, u32[]{:S(2)}) %collective-permute-start.7) | collective-permute-done | bytes 2208 | tf_op jit(solution)/shard_map/ppermute | solution.py:143
  92.0 2.0 %broadcast_in_dim.34.kappa_ref = f32[40,136,128]{2,1,0:T(8,128)} broadcast(f32[40,136]{1,0:T(8,128)S(1)} %pad_maximum_fusion.7), dimensions={0,1} | broadcast | bytes 2807040 | tf_op jit(solution)/shard_map/broadcast_in_dim | solution.py:195
  94.0 8.3 %forward.1 = f32[32,128,128]{2,1,0:T(8,128)} custom-call(f32[40,136,128]{2,1,0:T(8,128)} %pad_maximum_fusion.field_ref, f32[40,136,128]{2,1,0:T(8,128)} %broadcast_in_dim.34.kappa_ref), custom_call_target="tpu_custom_call" | custom-call | flops 27852800 | bytes 8355840 | tf_op jit(solution)/shard_map/forward/pallas_call | solution.py:200
  102.3 2.9 %convert_reduce_fusion.col_ref = s32[8192]{0:T(1024)} fusion(bf16[8192,128]{1,0:T(8,128)(2,1)S(1)} %bitcast.20), kind=kLoop, calls=%fused_computation | loop fusion | flops 40960 | bytes 65536 | tf_op jit(solution)/shard_map/convert_element_type | solution.py:192
  105.2 37.9 %observe.1 = f32[4096,128]{1,0:T(8,128)} custom-call(s32[8192]{0:T(1024)} %convert_reduce_fusion.col_ref, bf16[8192,128]{1,0:T(8,128)(2,1)} %bitcast.21, f32[4096,128]{1,0:T(8,128)} %bitcast.26), custom_call_target="tpu_custom_call" | custom-call | tf_op jit(solution)/shard_map/observe/pallas_call | solution.py:211
  143.1 1.9 %convert.10 = bf16[32,128,128]{2,1,0:T(8,128)(2,1)S(1)} convert(f32[32,128,128]{2,1,0:T(8,128)} %bitcast.22) | non-fusion elementwise | flops 524288 | bytes 3145728 | tf_op jit(solution)/shard_map/convert.5
  147.9 8.2 %collective-permute-done.9 = bf16[32,4,128]{2,1,0:T(4,128)(2,1)S(1)} collective-permute-done((bf16[32,4,128]{2,1,0:T(4,128)(2,1)S(1)}, bf16[32,4,128]{2,1,0:T(4,128)(2,1)S(1)}, u32[]{:S(2)}, u32[]{:S(2)}) %collective-permute-start.9) | collective-permute-done | bytes 32800 | tf_op jit(solution)/shard_map/ppermute | solution.py:142
  156.1 2.5 %collective-permute-start.10 = (bf16[4,136,128]{2,1,0:T(8,128)(2,1)S(1)}, bf16[4,136,128]{2,1,0:T(8,128)(2,1)S(1)}, u32[]{:S(2)}, u32[]{:S(2)}) collective-permute-start(bf16[4,136,128]{2,1,0:T(8,128)(2,1)S(1)} %get-tuple-element.5), channel_id=1, source_target_pairs={{0,8},{8,16},{16,24},{1,9},{9,17},{17,25},{2,10},{10,18},{18,26},{... | collective-permute-start | bytes 417800 | tf_op jit(solution)/shard_map/ppermute | solution.py:142
  158.6 2.1 %collective-permute-start.11 = (bf16[4,136,128]{2,1,0:T(8,128)(2,1)S(1)}, bf16[4,136,128]{2,1,0:T(8,128)(2,1)S(1)}, u32[]{:S(2)}, u32[]{:S(2)}) collective-permute-start(bf16[4,136,128]{2,1,0:T(8,128)(2,1)S(1)} %get-tuple-element.6), channel_id=1, source_target_pairs={{8,0},{16,8},{24,16},{9,1},{17,9},{25,17},{10,2},{18,10},{26,18},{... | collective-permute-start | bytes 417800 | tf_op jit(solution)/shard_map/ppermute | solution.py:143
  160.7 4.2 %collective-permute-done.11 = bf16[4,136,128]{2,1,0:T(8,128)(2,1)S(1)} collective-permute-done((bf16[4,136,128]{2,1,0:T(8,128)(2,1)S(1)}, bf16[4,136,128]{2,1,0:T(8,128)(2,1)S(1)}, u32[]{:S(2)}, u32[]{:S(2)}) %collective-permute-start.11) | collective-permute-done | bytes 139296 | tf_op jit(solution)/shard_map/ppermute | solution.py:143
  166.8 9.5 %adjoint.1 = f32[32,128,128]{2,1,0:T(8,128)} custom-call(f32[40,136,128]{2,1,0:T(8,128)} %pad_maximum_fusion.1.field_ref, f32[40,136,128]{2,1,0:T(8,128)} %broadcast_in_dim.34.kappa_ref), custom_call_target="tpu_custom_call" | custom-call | tf_op jit(solution)/shard_map/adjoint/pallas_call | solution.py:222
  176.3 4.6 %fusion.5 = f32[80,32,128]{2,0,1:T(8,128)S(1)} fusion(f32[32,128,128]{2,1,0:T(8,128)} %adjoint.1, f32[80,32,128]{2,1,0:T(8,128)S(1)} %copy-done.2, f32[80,80]{1,0:T(8,128)S(1)} %copy-done.4), kind=kOutput, calls=%fused_computation.7 | convolution fusion | flops 314900480 | bytes 4744192 | tf_op jit(solution)/shard_map/jk,abj->kab/dot_general | solution.py:231
  (41 shorter events, 13.1 us)
Async XLA Ops:
  21.1 7.1 %copy-start.4 = (f32[80,80]{1,0:T(8,128)S(1)}, f32[80,80]{1,0:T(8,128)}, u32[]{:S(2)}) copy-start(f32[80,80]{1,0:T(8,128)} %param.9) | copy-start | bytes 76804
  21.1 7.2 %copy-start.2 = (f32[80,32,128]{2,1,0:T(8,128)S(1)}, f32[80,32,128]{2,1,0:T(8,128)}, u32[]{:S(2)}) copy-start(f32[80,32,128]{2,1,0:T(8,128)} %param.8) | copy-start | bytes 3932164
  21.1 81.2 %all-to-all-start = ((bf16[32,256,128]{2,1,0:T(8,128)(2,1)}), bf16[32,256,128]{2,1,0:T(8,128)(2,1)S(1)}, u32[]{:S(2)}, u32[]{:S(2)}) async-start(bf16[32,256,128]{2,1,0:T(8,128)(2,1)} %bitcast.25), calls=%async_computation | async-start | bytes 4194304 | tf_op jit(solution)/shard_map/all_to_all | solution.py:183
  32.1 42.4 %copy-start.3 = (f32[32,128]{1,0:T(8,128)S(1)}, f32[32,128]{1,0:T(8,128)}, u32[]{:S(2)}) copy-start(f32[32,128]{1,0:T(8,128)} %param.10) | copy-start | bytes 49156
  32.1 32.0 %collective-permute-start = (f32[32,4,128]{2,1,0:T(4,128)S(1)}, f32[32,4,128]{2,1,0:T(4,128)S(1)}, u32[]{:S(2)}, u32[]{:S(2)}) collective-permute-start(f32[32,4,128]{2,1,0:T(4,128)S(1)} %get-tuple-element.9), channel_id=1, source_target_pairs={{1,0},{2,1},{3,2},{4,3},{5,4},{6,5},{7,6},{0,7},{9,8},{10,9},{11,1... | collective-permute-start | bytes 196616 | tf_op jit(solution)/shard_map/ppermute | solution.py:143
  36.4 32.3 %collective-permute-start.1 = (f32[32,4,128]{2,1,0:T(4,128)S(1)}, f32[32,4,128]{2,1,0:T(4,128)S(1)}, u32[]{:S(2)}, u32[]{:S(2)}) collective-permute-start(f32[32,4,128]{2,1,0:T(4,128)S(1)} %get-tuple-element.10), channel_id=1, source_target_pairs={{0,1},{1,2},{2,3},{3,4},{4,5},{5,6},{6,7},{7,0},{8,9},{9,10},{10,1... | collective-permute-start | bytes 196616 | tf_op jit(solution)/shard_map/ppermute | solution.py:142
  68.7 21.6 %collective-permute-start.2 = (f32[4,136,128]{2,1,0:T(8,128)S(1)}, f32[4,136,128]{2,1,0:T(8,128)S(1)}, u32[]{:S(2)}, u32[]{:S(2)}) collective-permute-start(f32[4,136,128]{2,1,0:T(8,128)S(1)} %get-tuple-element.7), channel_id=1, source_target_pairs={{0,8},{8,16},{16,24},{1,9},{9,17},{17,25},{2,10},{10,18},{18,26},{... | collective-permute-start | bytes 835592 | tf_op jit(solution)/shard_map/ppermute | solution.py:142
  72.6 17.6 %collective-permute-start.3 = (f32[4,136,128]{2,1,0:T(8,128)S(1)}, f32[4,136,128]{2,1,0:T(8,128)S(1)}, u32[]{:S(2)}, u32[]{:S(2)}) collective-permute-start(f32[4,136,128]{2,1,0:T(8,128)S(1)} %get-tuple-element.8), channel_id=1, source_target_pairs={{8,0},{16,8},{24,16},{9,1},{17,9},{25,17},{10,2},{18,10},{26,18},{... | collective-permute-start | bytes 835592 | tf_op jit(solution)/shard_map/ppermute | solution.py:143
  74.6 2.6 %collective-permute-start.4 = (f32[32,4]{1,0:T(8,128)S(1)}, f32[32,4]{1,0:T(8,128)S(1)}, u32[]{:S(2)}, u32[]{:S(2)}) collective-permute-start(f32[32,4]{1,0:T(8,128)S(1)} %get-tuple-element.15), channel_id=1, source_target_pairs={{1,0},{2,1},{3,2},{4,3},{5,4},{6,5},{7,6},{0,7},{9,8},{10,9},{11,1... | collective-permute-start | bytes 1544 | tf_op jit(solution)/shard_map/ppermute | solution.py:143
  74.8 5.3 %collective-permute-start.5 = (f32[32,4]{1,0:T(8,128)S(1)}, f32[32,4]{1,0:T(8,128)S(1)}, u32[]{:S(2)}, u32[]{:S(2)}) collective-permute-start(f32[32,4]{1,0:T(8,128)S(1)} %get-tuple-element.16), channel_id=1, source_target_pairs={{0,1},{1,2},{2,3},{3,4},{4,5},{5,6},{6,7},{7,0},{8,9},{9,10},{10,1... | collective-permute-start | bytes 1544 | tf_op jit(solution)/shard_map/ppermute | solution.py:142
  80.1 7.0 %collective-permute-start.6 = (f32[4,136]{1,0:T(4,128)S(1)}, f32[4,136]{1,0:T(4,128)S(1)}, u32[]{:S(2)}, u32[]{:S(2)}) collective-permute-start(f32[4,136]{1,0:T(4,128)S(1)} %get-tuple-element.13), channel_id=1, source_target_pairs={{0,8},{8,16},{16,24},{1,9},{9,17},{17,25},{2,10},{10,18},{18,26},{... | collective-permute-start | bytes 6536 | tf_op jit(solution)/shard_map/ppermute | solution.py:142
  85.2 4.9 %collective-permute-start.7 = (f32[4,136]{1,0:T(4,128)S(1)}, f32[4,136]{1,0:T(4,128)S(1)}, u32[]{:S(2)}, u32[]{:S(2)}) collective-permute-start(f32[4,136]{1,0:T(4,128)S(1)} %get-tuple-element.14), channel_id=1, source_target_pairs={{8,0},{16,8},{24,16},{9,1},{17,9},{25,17},{10,2},{18,10},{26,18},{... | collective-permute-start | bytes 6536 | tf_op jit(solution)/shard_map/ppermute | solution.py:143
  102.3 2.9 %copy-start = (bf16[32,256,128]{2,1,0:T(8,128)(2,1)}, bf16[32,256,128]{2,1,0:T(8,128)(2,1)S(1)}, u32[]{:S(2)}) copy-start(bf16[32,256,128]{2,1,0:T(8,128)(2,1)S(1)} %all-to-all-done) | copy-start | bytes 6291460
  143.1 13.0 %copy-start.1 = (f32[4096,128]{1,0:T(8,128)S(1)}, f32[4096,128]{1,0:T(8,128)}, u32[]{:S(2)}) copy-start(f32[4096,128]{1,0:T(8,128)} %observe.1) | copy-start | bytes 6291460
  145.0 2.8 %collective-permute-start.8 = (bf16[32,4,128]{2,1,0:T(4,128)(2,1)S(1)}, bf16[32,4,128]{2,1,0:T(4,128)(2,1)S(1)}, u32[]{:S(2)}, u32[]{:S(2)}) collective-permute-start(bf16[32,4,128]{2,1,0:T(4,128)(2,1)S(1)} %get-tuple-element.11), channel_id=1, source_target_pairs={{1,0},{2,1},{3,2},{4,3},{5,4},{6,5},{7,6},{0,7},{9,8},{10,9},{11,1... | collective-permute-start | bytes 98312 | tf_op jit(solution)/shard_map/ppermute | solution.py:143
  145.1 10.9 %collective-permute-start.9 = (bf16[32,4,128]{2,1,0:T(4,128)(2,1)S(1)}, bf16[32,4,128]{2,1,0:T(4,128)(2,1)S(1)}, u32[]{:S(2)}, u32[]{:S(2)}) collective-permute-start(bf16[32,4,128]{2,1,0:T(4,128)(2,1)S(1)} %get-tuple-element.12), channel_id=1, source_target_pairs={{0,1},{1,2},{2,3},{3,4},{4,5},{5,6},{6,7},{7,0},{8,9},{9,10},{10,1... | collective-permute-start | bytes 98312 | tf_op jit(solution)/shard_map/ppermute | solution.py:142
  156.1 4.6 %collective-permute-start.10 = (bf16[4,136,128]{2,1,0:T(8,128)(2,1)S(1)}, bf16[4,136,128]{2,1,0:T(8,128)(2,1)S(1)}, u32[]{:S(2)}, u32[]{:S(2)}) collective-permute-start(bf16[4,136,128]{2,1,0:T(8,128)(2,1)S(1)} %get-tuple-element.5), channel_id=1, source_target_pairs={{0,8},{8,16},{16,24},{1,9},{9,17},{17,25},{2,10},{10,18},{18,26},{... | collective-permute-start | bytes 417800 | tf_op jit(solution)/shard_map/ppermute | solution.py:142
  158.6 6.4 %collective-permute-start.11 = (bf16[4,136,128]{2,1,0:T(8,128)(2,1)S(1)}, bf16[4,136,128]{2,1,0:T(8,128)(2,1)S(1)}, u32[]{:S(2)}, u32[]{:S(2)}) collective-permute-start(bf16[4,136,128]{2,1,0:T(8,128)(2,1)S(1)} %get-tuple-element.6), channel_id=1, source_target_pairs={{8,0},{16,8},{24,16},{9,1},{17,9},{25,17},{10,2},{18,10},{26,18},{... | collective-permute-start | bytes 417800 | tf_op jit(solution)/shard_map/ppermute | solution.py:143
where the time goes:
time: 184 us; the launch traced here: 182 us
  Pallas kernels  66.3 us (36%)
  waiting for transfers between devices  52.9 us (29%)
  starting transfers between devices  31.7 us (17%)
  local copies, waits for them, and re-layouts  12.1 us (7%)
  other arithmetic  10.8 us (6%)
  matrix products  8.38 us (5%)
    pallas_call x1, Pallas kernels, local(): pl.pallas_call(functools.partial(obs_kernel, levels), out_shape=jax.Shape...  37.9 us
    ppermute x6, waiting for transfers between devices, exchange(): high = lax.ppermute(high, axis, backward).astype(block.dtype)  37.4 us
    ppermute x6, waiting for transfers between devices, exchange(): low = lax.ppermute(low, axis, forward).astype(block.dtype)  15.5 us
    ppermute x6, starting transfers between devices, exchange(): low = lax.ppermute(low, axis, forward).astype(block.dtype)  14.2 us
    pallas_call x1, Pallas kernels, local(): pl.pallas_call(pack_kernel, out_shape=jax.ShapeDtypeStruct((total, LANES)...  10.6 us
    ppermute x6, starting transfers between devices, exchange(): high = lax.ppermute(high, axis, backward).astype(block.dtype)  10.4 us
    pallas_call x1, Pallas kernels, local(): pl.pallas_call(adjoint_kernel, out_shape=jax.ShapeDtypeStruct((lat_rows,...  9.48 us
    concatenate x1, local copies, waits for them, and re-layouts, local(): jnp.concatenate([obs_weights.astype(f32), obs_values.astype(f32)[None], o...  8.31 us
  transfers between devices with their start and end apart: 13, of which 8 were waited for; matrix products, arithmetic and copies ran while one was open for 4% of the time, Pallas kernels for 5%

commit v1 on v0

--- a/solution.py
+++ b/solution.py
@@ -15,13 +15,19 @@
 PARAMS = pltpu.CompilerParams(vmem_limit_bytes=56 * 2**20)
 
 
-def pack_kernel(slot_ref, payload_ref, out_ref, rows, slots):
+def pack_kernel(slot_ref, weights_ref, extras_ref, out_ref, rows, slots):
     obs = rows.shape[0]
+    rest = LANES - weights_ref.shape[0] - extras_ref.shape[0]
 
     @pl.loop(0, obs // LANES)
     def _(j):
         at = pl.multiple_of(j * LANES, LANES)
-        rows[pl.ds(at, LANES), :] = payload_ref[:, pl.ds(at, LANES)].T
+        block = [
+            weights_ref[:, pl.ds(at, LANES)].astype(jnp.float32),
+            extras_ref[:, pl.ds(at, LANES)],
+            jnp.zeros((rest, LANES), jnp.float32),
+        ]
+        rows[pl.ds(at, LANES), :] = jnp.concatenate(block, axis=0).T
 
     @pl.loop(0, slots.shape[0] // 256)
     def _(j):
@@ -87,9 +93,15 @@
     return pltpu.roll(row, 1, 0) + pltpu.roll(row, width - 1, 0)
 
 
-def forward_kernel(field_ref, kappa_ref, out_ref, one, two):
+def forward_kernel(levels, field_ref, out_ref, kappa_ref, one, two):
     rows, lon = out_ref.shape[:2]
-    total = field_ref.shape[0]
+    total, width = field_ref.shape[:2]
+    kept = lax.broadcasted_iota(jnp.int32, (lon, LANES), 1) < levels
+
+    @pl.loop(0, total)
+    def _(r):
+        kappa_ref[r] = jnp.broadcast_to(field_ref[r][:, levels : levels + 1], (width, LANES))
+
     source = field_ref
     for step in range(NSTEP):
         last = step == NSTEP - 1
@@ -100,7 +112,7 @@
             f = source[r]
             new = f + kappa_ref[r] * (source[r - 1] + source[r + 1] + ring(f) - 4.0 * f)
             if last:
-                out_ref[r - NSTEP] = new[:lon]
+                out_ref[r - NSTEP] = jnp.where(kept, new[:lon], 0.0)
             else:
                 target[r] = new
 
@@ -160,26 +172,32 @@
     cells = lat_rows * lon_cells
     f32 = jnp.float32
 
-    payload = jnp.concatenate(
+    extras = jnp.stack(
         [
-            obs_weights.astype(f32),
-            obs_values.astype(f32)[None],
-            obs_precision.astype(f32)[None],
-            (obs_column // lon_cells).astype(f32)[None],
-            (obs_column % lon_cells).astype(f32)[None],
-            jnp.zeros((LANES - levels - 4, obs_here), f32),
-        ],
-        axis=0,
+            obs_values.astype(f32),
+            obs_precision.astype(f32),
+            (obs_column // lon_cells).astype(f32),
+            (obs_column % lon_cells).astype(f32),
+        ]
+        + [jnp.zeros((obs_here,), f32)] * 4
     )
     send = pl.pallas_call(
         pack_kernel,
         out_shape=jax.ShapeDtypeStruct((total, LANES), jnp.bfloat16),
-        in_specs=[SMEM, VMEM],
+        in_specs=[SMEM, VMEM, VMEM],
         out_specs=VMEM,
         scratch_shapes=[pltpu.VMEM((obs_here, LANES), f32), pltpu.VMEM((total, LANES), f32)],
         compiler_params=PARAMS,
+        cost_estimate=pl.CostEstimate(flops=0, bytes_accessed=30 * total * LANES, transcendentals=0),
         name="pack",
-    )(obs_slot, payload)
+    )(obs_slot, obs_weights, extras)
+    wide = jnp.pad(vertical, ((0, LANES - levels), (0, 0)))
+    start = jnp.einsum("kj,jab->abk", wide, control, precision=lax.Precision.HIGHEST)
+    start = start + kappa[:, :, None] * (jnp.arange(LANES) == levels).astype(f32)
+    low, high = exchange(start, "lon", 1, True, f32)
+    start = jnp.concatenate([start, high, low], axis=1)
+    low, high = exchange(start, "lat", 0, False, f32)
+    send, low, high = lax.optimization_barrier((send, low, high))
     got = lax.all_to_all(
         send.reshape(devices, slot_count, LANES),
         ("lat", "lon"),
@@ -190,23 +208,21 @@
     columns = (
         got[:, levels + 2].astype(f32) * lon_cells + got[:, levels + 3].astype(f32)
     ).astype(jnp.int32)
-
-    kappa_ext = extended(kappa, f32)
-    kappa_ext = jnp.broadcast_to(kappa_ext[:, :, None], kappa_ext.shape + (LANES,))
-    wide = jnp.pad(vertical, ((0, LANES - levels), (0, 0)))
-    start = jnp.einsum("kj,jab->abk", wide, control, precision=lax.Precision.HIGHEST)
-    start = extended(start, f32)
+    start = jnp.concatenate([low, start, high], axis=0)
     ext = start.shape
-    state = pl.pallas_call(
-        forward_kernel,
-        out_shape=jax.ShapeDtypeStruct((lat_rows, lon_cells, LANES), f32),
-        in_specs=[VMEM, VMEM],
-        out_specs=VMEM,
+    state, kappa_ext = pl.pallas_call(
+        functools.partial(forward_kernel, levels),
+        out_shape=(
+            jax.ShapeDtypeStruct((lat_rows, lon_cells, LANES), f32),
+            jax.ShapeDtypeStruct(ext, f32),
+        ),
+        in_specs=[VMEM],
+        out_specs=(VMEM, VMEM),
         scratch_shapes=[pltpu.VMEM(ext, f32), pltpu.VMEM(ext, f32)],
         compiler_params=PARAMS,
         cost_estimate=pl.CostEstimate(flops=40 * start.size, bytes_accessed=12 * start.size, transcendentals=0),
         name="forward",
-    )(start, kappa_ext)
+    )(start)
 
     adjoint = pl.pallas_call(
         functools.partial(obs_kernel, levels),

time: 184 us -> 165 us (0.90)
  starting transfers between devices: 31.7 us -> 22 us
  local copies, waits for them, and re-layouts: 12.1 us -> 3.19 us
  waiting for transfers between devices: 52.9 us -> 48.9 us
  Pallas kernels: 66.3 us -> 69.2 us
    all_to_all x1, waiting for transfers between devices: 0.01 us -> 34 us  [local(): lax.all_to_all(send.reshape(devices, slot_count, LANES), ('lat', 'lon'),...]
    ppermute x6 -> x4, waiting for transfers between devices: 37.4 us -> 6.86 us  [exchange(): high = lax.ppermute(high, axis, backward).astype(block.dtype)]
    concatenate x1 -> x0, local copies, waits for them, and re-layouts: 8.31 us -> none  [local(): jnp.concatenate([obs_weights.astype(f32), obs_values.astype(f32)[None], o...]
    ppermute x6 -> x4, waiting for transfers between devices: 15.5 us -> 8.08 us  [exchange(): low = lax.ppermute(low, axis, forward).astype(block.dtype)]
    ppermute x6 -> x4, starting transfers between devices: 14.2 us -> 9.35 us  [exchange(): low = lax.ppermute(low, axis, forward).astype(block.dtype)]
    all_to_all x1, starting transfers between devices: 7.1 us -> 2.48 us  [local(): lax.all_to_all(send.reshape(devices, slot_count, LANES), ('lat', 'lon'),...]
    pallas_call x1, Pallas kernels: 8.3 us -> 11.9 us  [local(): pl.pallas_call(functools.partial(forward_kernel, levels), out_shape=(jax....]
    concatenate x0 -> x2, other arithmetic: none -> 3.42 us  [the longest x1 3.38 us: local(): start = jnp.concatenate([low, start, high], axis=0)]
  transfers between devices with their start and end apart: 13 -> 9, of which waited for: 8 -> 6; matrix products, arithmetic and copies ran while one was open for 4% -> 3% of each run, Pallas kernels for 5% -> 13%
where the time goes in v1:
time: 165 us; the launch traced here: 164 us
  Pallas kernels  69.2 us (42%)
  waiting for transfers between devices  48.9 us (30%)
  starting transfers between devices  22 us (13%)
  other arithmetic  10.2 us (6%)
  matrix products  10.2 us (6%)
  local copies, waits for them, and re-layouts  3.19 us (2%)
    pallas_call x1, Pallas kernels, local(): pl.pallas_call(functools.partial(obs_kernel, levels), out_shape=jax.Shape...  37.6 us
    all_to_all x1, waiting for transfers between devices, local(): lax.all_to_all(send.reshape(devices, slot_count, LANES), ('lat', 'lon'),...  34 us
    pallas_call x1, Pallas kernels, local(): pl.pallas_call(functools.partial(forward_kernel, levels), out_shape=(jax....  11.9 us
    pallas_call x1, Pallas kernels, local(): pl.pallas_call(pack_kernel, out_shape=jax.ShapeDtypeStruct((total, LANES)...  10.2 us
    ppermute x4, starting transfers between devices, exchange(): high = lax.ppermute(high, axis, backward).astype(block.dtype)  10.1 us
    pallas_call x1, Pallas kernels, local(): pl.pallas_call(adjoint_kernel, out_shape=jax.ShapeDtypeStruct((lat_rows,...  9.57 us
    ppermute x4, starting transfers between devices, exchange(): low = lax.ppermute(low, axis, forward).astype(block.dtype)  9.35 us
    ppermute x4, waiting for transfers between devices, exchange(): low = lax.ppermute(low, axis, forward).astype(block.dtype)  8.08 us
  transfers between devices with their start and end apart: 9, of which 6 were waited for; matrix products, arithmetic and copies ran while one was open for 3% of the time, Pallas kernels for 13%

profile of v1, /device:TPU:1, one launch (start us, length us, event | category | flops | bytes accessed | tf_op | source)
XLA Modules:
  0.0 163.9 jit_solution(3221590891807725337)
XLA Ops:
  0.9 5.6 %bitcast_add_fusion = f32[32,128,128]{2,1,0:T(8,128)S(1)} fusion(f32[80,32,128]{2,1,0:T(8,128)} %param.8, f32[128]{0:T(128)S(1)} %compare_convert_fusion, f32[32,128]{1,0:T(8,128)} %param.10, f32[80,80]{0,1:T(8,128)S(1)} %copy.21), kind=kOutput, calls=%fused_computation.5 | convolution fusion | flops 504365056 | bytes 3450368 | tf_op jit(solution)/shard_map/kj,jab->abk/dot_general | solution.py:195
  6.5 5.2 %collective-permute-start = (f32[32,4,128]{2,1,0:T(4,128)S(1)}, f32[32,4,128]{2,1,0:T(4,128)S(1)}, u32[]{:S(2)}, u32[]{:S(2)}) collective-permute-start(f32[32,4,128]{2,1,0:T(4,128)S(1)} %get-tuple-element.19), channel_id=1, source_target_pairs={{1,0},{2,1},{3,2},{4,3},{5,4},{6,5},{7,6},{0,7},{9,8},{10,9},{11,1... | collective-permute-start | bytes 196616 | tf_op jit(solution)/shard_map/ppermute | solution.py:155
  11.7 1.3 collective-permute-done
  13.0 4.5 %collective-permute-done.1 = f32[32,4,128]{2,1,0:T(4,128)S(1)} collective-permute-done((f32[32,4,128]{2,1,0:T(4,128)S(1)}, f32[32,4,128]{2,1,0:T(4,128)S(1)}, u32[]{:S(2)}, u32[]{:S(2)}) %collective-permute-start.1) | collective-permute-done | bytes 65568 | tf_op jit(solution)/shard_map/ppermute | solution.py:154
  17.6 5.1 %collective-permute-start.2 = (f32[4,136,128]{2,1,0:T(8,128)S(1)}, f32[4,136,128]{2,1,0:T(8,128)S(1)}, u32[]{:S(2)}, u32[]{:S(2)}) collective-permute-start(f32[4,136,128]{2,1,0:T(8,128)S(1)} %get-tuple-element.18), channel_id=1, source_target_pairs={{0,8},{8,16},{16,24},{1,9},{9,17},{17,25},{2,10},{10,18},{18,26},{... | collective-permute-start | bytes 835592 | tf_op jit(solution)/shard_map/ppermute | solution.py:154
  22.7 1.9 %collective-permute-start.3 = (f32[4,136,128]{2,1,0:T(8,128)S(1)}, f32[4,136,128]{2,1,0:T(8,128)S(1)}, u32[]{:S(2)}, u32[]{:S(2)}) collective-permute-start(f32[4,136,128]{2,1,0:T(8,128)S(1)} %get-tuple-element.17), channel_id=1, source_target_pairs={{8,0},{16,8},{24,16},{9,1},{17,9},{25,17},{10,2},{18,10},{26,18},{... | collective-permute-start | bytes 835592 | tf_op jit(solution)/shard_map/ppermute | solution.py:155
  25.5 10.2 %pack.1 = bf16[8192,128]{1,0:T(8,128)(2,1)} custom-call(s32[4096]{0:T(1024)} %slot_ref.1, bf16[80,4096]{1,0:T(8,128)(2,1)} %weights_ref.1, f32[8,4096]{1,0:T(8,128)} %stack.31.extras_ref), custom_call_target="tpu_custom_call" | custom-call | bytes 31457280 | tf_op jit(solution)/shard_map/pack/pallas_call | solution.py:184
  35.6 2.5 %all-to-all-start = ((bf16[32,256,128]{2,1,0:T(8,128)(2,1)}), bf16[32,256,128]{2,1,0:T(8,128)(2,1)S(1)}, u32[]{:S(2)}, u32[]{:S(2)}) async-start(bf16[32,256,128]{2,1,0:T(8,128)(2,1)} %bitcast.25), calls=%async_computation | async-start | bytes 4194304 | tf_op jit(solution)/shard_map/all_to_all | solution.py:201
  38.1 3.4 %pad_maximum_fusion.field_ref = f32[40,136,128]{2,1,0:T(8,128)} fusion(f32[4,136,128]{2,1,0:T(8,128)S(1)} %collective-permute-done.3, f32[32,4,128]{2,1,0:T(4,128)S(1)} %collective-permute-done.1, f32[32,4,128]{2,1,0:T(4,128)S(1)} %collective-permute-done, f32[32,128,128]{2,1,0:T(8,128)} %copy-done.2, f32[4,136,128]{2,1,0:T(8,128)S(1)} %collective-permute-done.2), kind=kLoop, calls=%fused_computation.1 | loop fusion | flops 2785280 | bytes 5570560 | tf_op jit(solution)/shard_map/concatenate | solution.py:211
  41.5 11.9 %forward.1 = (f32[32,128,128]{2,1,0:T(8,128)}, f32[40,136,128]{2,1,0:T(8,128)}) custom-call(f32[40,136,128]{2,1,0:T(8,128)} %pad_maximum_fusion.field_ref), custom_call_target="tpu_custom_call" | custom-call | flops 27852800 | bytes 8355840 | tf_op jit(solution)/shard_map/forward/pallas_call | solution.py:213
  53.4 34.0 %all-to-all-done = bf16[32,256,128]{2,1,0:T(8,128)(2,1)S(1)} async-done(((bf16[32,256,128]{2,1,0:T(8,128)(2,1)}), bf16[32,256,128]{2,1,0:T(8,128)(2,1)S(1)}, u32[]{:S(2)}, u32[]{:S(2)}) %all-to-all-start) | async-done | bytes 2097184 | tf_op jit(solution)/shard_map/all_to_all | solution.py:201
  87.4 2.9 %convert_reduce_fusion.col_ref = s32[8192]{0:T(1024)} fusion(bf16[8192,128]{1,0:T(8,128)(2,1)S(1)} %bitcast.23), kind=kLoop, calls=%fused_computation | loop fusion | flops 40960 | bytes 65536 | tf_op jit(solution)/shard_map/convert_element_type | solution.py:210
  90.3 37.6 %observe.1 = f32[4096,128]{1,0:T(8,128)} custom-call(s32[8192]{0:T(1024)} %convert_reduce_fusion.col_ref, bf16[8192,128]{1,0:T(8,128)(2,1)} %bitcast.24, f32[4096,128]{1,0:T(8,128)} %bitcast.26), custom_call_target="tpu_custom_call" | custom-call | tf_op jit(solution)/shard_map/observe/pallas_call | solution.py:227
  127.9 1.9 %convert.10 = bf16[32,128,128]{2,1,0:T(8,128)(2,1)S(1)} convert(f32[32,128,128]{2,1,0:T(8,128)} %bitcast.20) | non-fusion elementwise | flops 524288 | bytes 3145728 | tf_op jit(solution)/shard_map/convert.5
  129.8 1.0 collective-permute-start.4
  131.4 1.3 collective-permute-done.4
  132.7 3.6 %collective-permute-done.5 = bf16[32,4,128]{2,1,0:T(4,128)(2,1)S(1)} collective-permute-done((bf16[32,4,128]{2,1,0:T(4,128)(2,1)S(1)}, bf16[32,4,128]{2,1,0:T(4,128)(2,1)S(1)}, u32[]{:S(2)}, u32[]{:S(2)}) %collective-permute-start.5) | collective-permute-done | bytes 32800 | tf_op jit(solution)/shard_map/ppermute | solution.py:154
  136.3 3.7 %collective-permute-start.6 = (bf16[4,136,128]{2,1,0:T(8,128)(2,1)S(1)}, bf16[4,136,128]{2,1,0:T(8,128)(2,1)S(1)}, u32[]{:S(2)}, u32[]{:S(2)}) collective-permute-start(bf16[4,136,128]{2,1,0:T(8,128)(2,1)S(1)} %get-tuple-element.15), channel_id=1, source_target_pairs={{0,8},{8,16},{16,24},{1,9},{9,17},{17,25},{2,10},{10,18},{18,26},{... | collective-permute-start | bytes 417800 | tf_op jit(solution)/shard_map/ppermute | solution.py:154
  140.0 2.1 %collective-permute-start.7 = (bf16[4,136,128]{2,1,0:T(8,128)(2,1)S(1)}, bf16[4,136,128]{2,1,0:T(8,128)(2,1)S(1)}, u32[]{:S(2)}, u32[]{:S(2)}) collective-permute-start(bf16[4,136,128]{2,1,0:T(8,128)(2,1)S(1)} %get-tuple-element.16), channel_id=1, source_target_pairs={{8,0},{16,8},{24,16},{9,1},{17,9},{25,17},{10,2},{18,10},{26,18},{... | collective-permute-start | bytes 417800 | tf_op jit(solution)/shard_map/ppermute | solution.py:155
  142.2 4.2 %collective-permute-done.7 = bf16[4,136,128]{2,1,0:T(8,128)(2,1)S(1)} collective-permute-done((bf16[4,136,128]{2,1,0:T(8,128)(2,1)S(1)}, bf16[4,136,128]{2,1,0:T(8,128)(2,1)S(1)}, u32[]{:S(2)}, u32[]{:S(2)}) %collective-permute-start.7) | collective-permute-done | bytes 139296 | tf_op jit(solution)/shard_map/ppermute | solution.py:155
  146.4 1.8 %pad_maximum_fusion.1.field_ref = f32[40,136,128]{2,1,0:T(8,128)} fusion(f32[4,136,128]{2,1,0:T(8,128)S(1)} %convert_element_type.56, f32[32,4,128]{2,1,0:T(4,128)S(1)} %convert_element_type.54, f32[32,4,128]{2,1,0:T(4,128)S(1)} %convert_element_type.53, f32[32,128,128]{2,1,0:T(8,128)S(1)} %bitcast.22, f32[4,136,128]{2,1,0:T(8,128)S(1)} %convert_element_type.55), kind=kLoop, calls=%fused_computation.2 | loop fusion | flops 2785280 | bytes 5570560 | tf_op jit(solution)/shard_map/concatenate | solution.py:163
  148.2 9.6 %adjoint.1 = f32[32,128,128]{2,1,0:T(8,128)} custom-call(f32[40,136,128]{2,1,0:T(8,128)} %pad_maximum_fusion.1.field_ref, f32[40,136,128]{2,1,0:T(8,128)} %get-tuple-element.14.kappa_ref), custom_call_target="tpu_custom_call" | custom-call | tf_op jit(solution)/shard_map/adjoint/pallas_call | solution.py:238
  157.8 4.6 %fusion.5 = f32[80,32,128]{2,0,1:T(8,128)S(1)} fusion(f32[32,128,128]{2,1,0:T(8,128)} %adjoint.1, f32[80,32,128]{2,1,0:T(8,128)S(1)} %copy-done.3, f32[80,80]{1,0:T(8,128)S(1)} %copy-done.4), kind=kOutput, calls=%fused_computation.7 | convolution fusion | flops 314900480 | bytes 4744192 | tf_op jit(solution)/shard_map/jk,abj->kab/dot_general | solution.py:247
  162.4 1.5 copy.26
  (36 shorter events, 2.5 us)
Async XLA Ops:
  6.5 11.1 %copy-start.2 = (f32[32,128,128]{2,1,0:T(8,128)}, f32[32,128,128]{2,1,0:T(8,128)S(1)}, u32[]{:S(2)}) copy-start(f32[32,128,128]{2,1,0:T(8,128)S(1)} %bitcast_add_fusion) | copy-start | bytes 6291460
  6.5 18.1 %copy-start.6 = (bf16[4096]{0:T(1024)(128)(2,1)S(1)}, bf16[4096]{0:T(1024)(128)(2,1)}, u32[]{:S(2)}) copy-start(bf16[4096]{0:T(1024)(128)(2,1)} %param.12) | copy-start | bytes 24580
  6.5 18.2 %copy-start.7 = (bf16[4096]{0:T(1024)(128)(2,1)S(1)}, bf16[4096]{0:T(1024)(128)(2,1)}, u32[]{:S(2)}) copy-start(bf16[4096]{0:T(1024)(128)(2,1)} %param.13) | copy-start | bytes 24580
  6.5 18.2 %copy-start.5 = (s32[4096]{0:T(1024)S(1)}, s32[4096]{0:T(1024)}, u32[]{:S(2)}) copy-start(s32[4096]{0:T(1024)} %param.15) | copy-start | bytes 49156
  6.5 6.5 %collective-permute-start = (f32[32,4,128]{2,1,0:T(4,128)S(1)}, f32[32,4,128]{2,1,0:T(4,128)S(1)}, u32[]{:S(2)}, u32[]{:S(2)}) collective-permute-start(f32[32,4,128]{2,1,0:T(4,128)S(1)} %get-tuple-element.19), channel_id=1, source_target_pairs={{1,0},{2,1},{3,2},{4,3},{5,4},{6,5},{7,6},{0,7},{9,8},{10,9},{11,1... | collective-permute-start | bytes 196616 | tf_op jit(solution)/shard_map/ppermute | solution.py:155
  11.7 5.8 %collective-permute-start.1 = (f32[32,4,128]{2,1,0:T(4,128)S(1)}, f32[32,4,128]{2,1,0:T(4,128)S(1)}, u32[]{:S(2)}, u32[]{:S(2)}) collective-permute-start(f32[32,4,128]{2,1,0:T(4,128)S(1)} %get-tuple-element.20), channel_id=1, source_target_pairs={{0,1},{1,2},{2,3},{3,4},{4,5},{5,6},{6,7},{7,0},{8,9},{9,10},{10,1... | collective-permute-start | bytes 196616 | tf_op jit(solution)/shard_map/ppermute | solution.py:154
  17.6 18.1 %collective-permute-start.2 = (f32[4,136,128]{2,1,0:T(8,128)S(1)}, f32[4,136,128]{2,1,0:T(8,128)S(1)}, u32[]{:S(2)}, u32[]{:S(2)}) collective-permute-start(f32[4,136,128]{2,1,0:T(8,128)S(1)} %get-tuple-element.18), channel_id=1, source_target_pairs={{0,8},{8,16},{16,24},{1,9},{9,17},{17,25},{2,10},{10,18},{18,26},{... | collective-permute-start | bytes 835592 | tf_op jit(solution)/shard_map/ppermute | solution.py:154
  22.7 13.0 %collective-permute-start.3 = (f32[4,136,128]{2,1,0:T(8,128)S(1)}, f32[4,136,128]{2,1,0:T(8,128)S(1)}, u32[]{:S(2)}, u32[]{:S(2)}) collective-permute-start(f32[4,136,128]{2,1,0:T(8,128)S(1)} %get-tuple-element.17), channel_id=1, source_target_pairs={{8,0},{16,8},{24,16},{9,1},{17,9},{25,17},{10,2},{18,10},{26,18},{... | collective-permute-start | bytes 835592 | tf_op jit(solution)/shard_map/ppermute | solution.py:155
  35.6 51.7 %all-to-all-start = ((bf16[32,256,128]{2,1,0:T(8,128)(2,1)}), bf16[32,256,128]{2,1,0:T(8,128)(2,1)S(1)}, u32[]{:S(2)}, u32[]{:S(2)}) async-start(bf16[32,256,128]{2,1,0:T(8,128)(2,1)} %bitcast.25), calls=%async_computation | async-start | bytes 4194304 | tf_op jit(solution)/shard_map/all_to_all | solution.py:201
  87.4 2.9 %copy-start.1 = (bf16[32,256,128]{2,1,0:T(8,128)(2,1)}, bf16[32,256,128]{2,1,0:T(8,128)(2,1)S(1)}, u32[]{:S(2)}) copy-start(bf16[32,256,128]{2,1,0:T(8,128)(2,1)S(1)} %all-to-all-done) | copy-start | bytes 6291460
  127.9 8.4 %copy-start = (f32[4096,128]{1,0:T(8,128)S(1)}, f32[4096,128]{1,0:T(8,128)}, u32[]{:S(2)}) copy-start(f32[4096,128]{1,0:T(8,128)} %observe.1) | copy-start | bytes 6291460
  129.8 2.8 %collective-permute-start.4 = (bf16[32,4,128]{2,1,0:T(4,128)(2,1)S(1)}, bf16[32,4,128]{2,1,0:T(4,128)(2,1)S(1)}, u32[]{:S(2)}, u32[]{:S(2)}) collective-permute-start(bf16[32,4,128]{2,1,0:T(4,128)(2,1)S(1)} %get-tuple-element.21), channel_id=1, source_target_pairs={{1,0},{2,1},{3,2},{4,3},{5,4},{6,5},{7,6},{0,7},{9,8},{10,9},{11,1... | collective-permute-start | bytes 98312 | tf_op jit(solution)/shard_map/ppermute | solution.py:155
  130.8 5.5 %collective-permute-start.5 = (bf16[32,4,128]{2,1,0:T(4,128)(2,1)S(1)}, bf16[32,4,128]{2,1,0:T(4,128)(2,1)S(1)}, u32[]{:S(2)}, u32[]{:S(2)}) collective-permute-start(bf16[32,4,128]{2,1,0:T(4,128)(2,1)S(1)} %get-tuple-element.22), channel_id=1, source_target_pairs={{0,1},{1,2},{2,3},{3,4},{4,5},{5,6},{6,7},{7,0},{8,9},{9,10},{10,1... | collective-permute-start | bytes 98312 | tf_op jit(solution)/shard_map/ppermute | solution.py:154
  136.3 5.8 %collective-permute-start.6 = (bf16[4,136,128]{2,1,0:T(8,128)(2,1)S(1)}, bf16[4,136,128]{2,1,0:T(8,128)(2,1)S(1)}, u32[]{:S(2)}, u32[]{:S(2)}) collective-permute-start(bf16[4,136,128]{2,1,0:T(8,128)(2,1)S(1)} %get-tuple-element.15), channel_id=1, source_target_pairs={{0,8},{8,16},{16,24},{1,9},{9,17},{17,25},{2,10},{10,18},{18,26},{... | collective-permute-start | bytes 417800 | tf_op jit(solution)/shard_map/ppermute | solution.py:154
  140.0 6.4 %collective-permute-start.7 = (bf16[4,136,128]{2,1,0:T(8,128)(2,1)S(1)}, bf16[4,136,128]{2,1,0:T(8,128)(2,1)S(1)}, u32[]{:S(2)}, u32[]{:S(2)}) collective-permute-start(bf16[4,136,128]{2,1,0:T(8,128)(2,1)S(1)} %get-tuple-element.16), channel_id=1, source_target_pairs={{8,0},{16,8},{24,16},{9,1},{17,9},{25,17},{10,2},{18,10},{26,18},{... | collective-permute-start | bytes 417800 | tf_op jit(solution)/shard_map/ppermute | solution.py:155
  148.2 9.6 %copy-start.3 = (f32[80,32,128]{2,1,0:T(8,128)S(1)}, f32[80,32,128]{2,1,0:T(8,128)}, u32[]{:S(2)}) copy-start(f32[80,32,128]{2,1,0:T(8,128)} %param.8) | copy-start | bytes 3932164
  148.2 9.6 %copy-start.4 = (f32[80,80]{1,0:T(8,128)S(1)}, f32[80,80]{1,0:T(8,128)}, u32[]{:S(2)}) copy-start(f32[80,80]{1,0:T(8,128)} %param.9) | copy-start | bytes 76804

commit v2 on v1

--- a/solution.py
+++ b/solution.py
@@ -13,6 +13,15 @@
 VMEM = pl.BlockSpec(memory_space=pltpu.VMEM)
 SMEM = pl.BlockSpec(memory_space=pltpu.SMEM)
 PARAMS = pltpu.CompilerParams(vmem_limit_bytes=56 * 2**20)
+
+
+HEAD = 64
+
+
+def packing(levels, slot_count):
+    tail = levels + 4 - HEAD
+    beside = LANES // tail
+    return tail, beside, -(-slot_count // (16 * beside)) * 16
 
 
 def pack_kernel(slot_ref, weights_ref, extras_ref, out_ref, rows, slots):
@@ -40,15 +49,64 @@
         for u in range(32):
             slots[pl.ds(slot_ref[at + u], 1), :] = rows[pl.ds(at + u, 1), :]
 
-    @pl.loop(0, slots.shape[0] // 256)
-    def _(j):
-        at = pl.multiple_of(j * 256, 256)
-        out_ref[pl.ds(at, 256), :] = slots[pl.ds(at, 256), :].astype(jnp.bfloat16)
-
-
-def obs_kernel(levels, col_ref, got_ref, state_ref, out_ref, picked, *sums):
-    count = picked.shape[0]
+    owners = out_ref.shape[0]
+    count = slots.shape[0] // owners
+    half = count // 2
+    tail, beside, group = packing(weights_ref.shape[0], count)
+    head_lane = lax.broadcasted_iota(jnp.int32, (half, LANES), 1)
+    tail_lane = lax.broadcasted_iota(jnp.int32, (group, LANES), 1)
+
+    @pl.loop(0, owners)
+    def _(o):
+        at = pl.multiple_of(o * count, count)
+        second = pltpu.roll(slots[pl.ds(at + half, half), :], HEAD, 1)
+        head = jnp.where(head_lane < HEAD, slots[pl.ds(at, half), :], second)
+        out_ref[o, :half, :] = head.astype(jnp.bfloat16)
+        tails = jnp.zeros((group, LANES), jnp.float32)
+        for g in range(beside):
+            size = min(group, count - g * group)
+            if size <= 0:
+                continue
+            rest_rows = slots[pl.ds(at + g * group, size), :]
+            if size < group:
+                rest_rows = jnp.concatenate([rest_rows, jnp.zeros((group - size, LANES), jnp.float32)], axis=0)
+            moved = pltpu.roll(rest_rows, (tail * g - HEAD) % LANES, 1)
+            tails = jnp.where((tail_lane >= tail * g) & (tail_lane < tail * (g + 1)), moved, tails)
+        out_ref[o, half:, :] = tails.astype(jnp.bfloat16)
+
+
+def obs_kernel(levels, lon_cells, got_ref, state_ref, out_ref, picked, weights, cols, col_ref, sem, *sums):
     cells = state_ref.shape[0]
+    owners, slot_count = cols.shape
+    half = slot_count // 2
+    tail, beside, group = packing(levels, slot_count)
+    unroll = min(slot_count, 32)
+    lane = lax.broadcasted_iota(jnp.int32, (8, LANES), 1)
+    scale = jnp.where(lane == levels + 2, float(lon_cells), jnp.where(lane == levels + 3, 1.0, 0.0))
+    scale = scale.astype(jnp.bfloat16)
+
+    @pl.loop(0, owners)
+    def _(o):
+        at = pl.multiple_of(o * slot_count, slot_count)
+        head = got_ref[o, :half, :].astype(jnp.float32)
+        tails = got_ref[o, half:, :].astype(jnp.float32)
+        heads = jnp.concatenate([head, pltpu.roll(head, HEAD, 1)], axis=0)
+        parts = []
+        for g in range(beside):
+            size = min(group, slot_count - g * group)
+            if size > 0:
+                parts.append(pltpu.roll(tails[:size], (HEAD - tail * g) % LANES, 1))
+        rest = jnp.concatenate(parts, axis=0)
+        which = lax.broadcasted_iota(jnp.int32, (slot_count, LANES), 1)
+        rows = jnp.where(which < HEAD, heads, rest)
+        weights[pl.ds(at, slot_count), :] = rows
+        column = lax.dot_general(
+            scale, rows.astype(jnp.bfloat16), (((1,), (1,)), ((), ())), preferred_element_type=jnp.float32
+        )
+        cols[pl.ds(o, 1), :] = column[:1].astype(jnp.int32)
+
+    copy = pltpu.make_async_copy(cols, col_ref, sem)
+    copy.start()
 
     @pl.loop(0, cells // 256)
     def _(j):
@@ -56,28 +114,34 @@
         for s in sums:
             s[pl.ds(at, 256), :] = jnp.zeros((256, LANES), jnp.float32)
 
-    @pl.loop(0, count // 32)
-    def _(j):
-        at = pl.multiple_of(j * 32, 32)
-        for u in range(32):
-            picked[pl.ds(at + u, 1), :] = state_ref[pl.ds(col_ref[at + u], 1), :]
-
-    @pl.loop(0, count // 128)
+    copy.wait()
+
+    @pl.loop(0, owners)
+    def _(o):
+        @pl.loop(0, slot_count // unroll)
+        def _(j):
+            at = pl.multiple_of(o * slot_count + j * unroll, unroll)
+            for u in range(unroll):
+                picked[pl.ds(at + u, 1), :] = state_ref[pl.ds(col_ref[o, j * unroll + u], 1), :]
+
+    @pl.loop(0, owners * slot_count // 128)
     def _(j):
         at = pl.multiple_of(j * 128, 128)
-        w = got_ref[pl.ds(at, 128), :].astype(jnp.float32)
+        w = weights[pl.ds(at, 128), :]
         model = jnp.sum(w * picked[pl.ds(at, 128), :], axis=1, keepdims=True)
         weighted = w[:, levels + 1 : levels + 2] * (model - w[:, levels : levels + 1])
         picked[pl.ds(at, 128), :] = w * weighted
 
-    @pl.loop(0, count // 32)
-    def _(j):
-        at = pl.multiple_of(j * 32, 32)
-        for u in range(0, 32, CHAINS):
-            cols = [col_ref[at + u + c] for c in range(CHAINS)]
-            old = [sums[c][pl.ds(cols[c], 1), :] for c in range(CHAINS)]
-            for c in range(CHAINS):
-                sums[c][pl.ds(cols[c], 1), :] = old[c] + picked[pl.ds(at + u + c, 1), :]
+    @pl.loop(0, owners)
+    def _(o):
+        @pl.loop(0, slot_count // unroll)
+        def _(j):
+            at = pl.multiple_of(o * slot_count + j * unroll, unroll)
+            for u in range(0, unroll, CHAINS):
+                where = [col_ref[o, j * unroll + u + c] for c in range(CHAINS)]
+                old = [sums[c][pl.ds(where[c], 1), :] for c in range(CHAINS)]
+                for c in range(CHAINS):
+                    sums[c][pl.ds(where[c], 1), :] = old[c] + picked[pl.ds(at + u + c, 1), :]
 
     @pl.loop(0, cells // 64)
     def _(j):
@@ -181,9 +245,10 @@
         ]
         + [jnp.zeros((obs_here,), f32)] * 4
     )
+    packed = slot_count // 2 + packing(levels, slot_count)[2]
     send = pl.pallas_call(
         pack_kernel,
-        out_shape=jax.ShapeDtypeStruct((total, LANES), jnp.bfloat16),
+        out_shape=jax.ShapeDtypeStruct((devices, packed, LANES), jnp.bfloat16),
         in_specs=[SMEM, VMEM, VMEM],
         out_specs=VMEM,
         scratch_shapes=[pltpu.VMEM((obs_here, LANES), f32), pltpu.VMEM((total, LANES), f32)],
@@ -198,16 +263,7 @@
     start = jnp.concatenate([start, high, low], axis=1)
     low, high = exchange(start, "lat", 0, False, f32)
     send, low, high = lax.optimization_barrier((send, low, high))
-    got = lax.all_to_all(
-        send.reshape(devices, slot_count, LANES),
-        ("lat", "lon"),
-        split_axis=0,
-        concat_axis=0,
-        tiled=True,
-    ).reshape(total, LANES)
-    columns = (
-        got[:, levels + 2].astype(f32) * lon_cells + got[:, levels + 3].astype(f32)
-    ).astype(jnp.int32)
+    got = lax.all_to_all(send, ("lat", "lon"), split_axis=0, concat_axis=0, tiled=True)
     start = jnp.concatenate([low, start, high], axis=0)
     ext = start.shape
     state, kappa_ext = pl.pallas_call(
@@ -225,14 +281,21 @@
     )(start)
 
     adjoint = pl.pallas_call(
-        functools.partial(obs_kernel, levels),
+        functools.partial(obs_kernel, levels, lon_cells),
         out_shape=jax.ShapeDtypeStruct((cells, LANES), f32),
-        in_specs=[SMEM, VMEM, VMEM],
+        in_specs=[VMEM, VMEM],
         out_specs=VMEM,
-        scratch_shapes=[pltpu.VMEM((total, LANES), f32)] + [pltpu.VMEM((cells, LANES), f32)] * CHAINS,
+        scratch_shapes=[
+            pltpu.VMEM((total, LANES), f32),
+            pltpu.VMEM((total, LANES), f32),
+            pltpu.VMEM((devices, slot_count), jnp.int32),
+            pltpu.SMEM((devices, slot_count), jnp.int32),
+            pltpu.SemaphoreType.DMA,
+        ]
+        + [pltpu.VMEM((cells, LANES), f32)] * CHAINS,
         compiler_params=PARAMS,
         name="observe",
-    )(columns, got, state.reshape(cells, LANES))
+    )(got, state.reshape(cells, LANES))
 
     adjoint = extended(adjoint.reshape(lat_rows, lon_cells, LANES), jnp.bfloat16)
     adjoint = pl.pallas_call(

time: 165 us -> 187 us (1.13)
  Pallas kernels: 69.2 us -> 106 us
  waiting for transfers between devices: 48.9 us -> 35.4 us
  other arithmetic: 10.2 us -> 6.74 us
  local copies, waits for them, and re-layouts: 3.19 us -> 5.73 us
    pallas_call x2, Pallas kernels: 47.7 us -> 84.5 us  [the longest x1 71.6 us: local(): pl.pallas_call(functools.partial(obs_kernel, levels, lon_cells), out_shap...]
    all_to_all x1, waiting for transfers between devices: 34 us -> 20.2 us  [local(): lax.all_to_all(send, ('lat', 'lon'), split_axis=0, concat_axis=0, tiled=T...]
    convert_element_type x1 -> x0, other arithmetic: 2.92 us -> none  [local(): columns = (got[:, levels + 2].astype(f32) * lon_cells + got[:, levels + 3...]
    unnamed x17 -> x23, local copies, waits for them, and re-layouts: 0.89 us -> 3.43 us
    ppermute x4, starting transfers between devices: 10.1 us -> 12 us  [exchange(): high = lax.ppermute(high, axis, backward).astype(block.dtype)]
  transfers between devices with their start and end apart: 9 -> 9, of which waited for: 6 -> 7; matrix products, arithmetic and copies ran while one was open for 3% -> 2% of each run, Pallas kernels for 13% -> 13%
where the time goes in v2:
time: 187 us; the launch traced here: 186 us
  Pallas kernels  106 us (57%)
  waiting for transfers between devices  35.4 us (19%)
  starting transfers between devices  22.3 us (12%)
  matrix products  10.1 us (5%)
  other arithmetic  6.74 us (4%)
  local copies, waits for them, and re-layouts  5.73 us (3%)
    pallas_call x1, Pallas kernels, local(): pl.pallas_call(functools.partial(obs_kernel, levels, lon_cells), out_shap...  71.6 us
    all_to_all x1, waiting for transfers between devices, local(): lax.all_to_all(send, ('lat', 'lon'), split_axis=0, concat_axis=0, tiled=T...  20.2 us
    pallas_call x1, Pallas kernels, local(): pl.pallas_call(pack_kernel, out_shape=jax.ShapeDtypeStruct((devices, pack...  12.9 us
    ppermute x4, starting transfers between devices, exchange(): high = lax.ppermute(high, axis, backward).astype(block.dtype)  12 us
    pallas_call x1, Pallas kernels, local(): pl.pallas_call(functools.partial(forward_kernel, levels), out_shape=(jax....  11.7 us
    pallas_call x1, Pallas kernels, local(): pl.pallas_call(adjoint_kernel, out_shape=jax.ShapeDtypeStruct((lat_rows,...  9.57 us
    ppermute x4, waiting for transfers between devices, exchange(): low = lax.ppermute(low, axis, forward).astype(block.dtype)  8.14 us
    ppermute x4, starting transfers between devices, exchange(): low = lax.ppermute(low, axis, forward).astype(block.dtype)  7.89 us
  transfers between devices with their start and end apart: 9, of which 7 were waited for; matrix products, arithmetic and copies ran while one was open for 2% of the time, Pallas kernels for 13%

profile of v2, /device:TPU:1, one launch (start us, length us, event | category | flops | bytes accessed | tf_op | source)
XLA Modules:
  0.0 186.3 jit_solution(7790846102928907950)
XLA Ops:
  0.9 5.5 %bitcast_add_fusion = f32[32,128,128]{2,1,0:T(8,128)S(1)} fusion(f32[80,32,128]{2,1,0:T(8,128)} %param.8, f32[128]{0:T(128)S(1)} %compare_convert_fusion, f32[32,128]{1,0:T(8,128)} %param.10, f32[80,80]{0,1:T(8,128)S(1)} %copy.9), kind=kOutput, calls=%fused_computation.4 | convolution fusion | flops 504365056 | bytes 3450368 | tf_op jit(solution)/shard_map/kj,jab->abk/dot_general | solution.py:260
  6.4 5.2 %collective-permute-start = (f32[32,4,128]{2,1,0:T(4,128)S(1)}, f32[32,4,128]{2,1,0:T(4,128)S(1)}, u32[]{:S(2)}, u32[]{:S(2)}) collective-permute-start(f32[32,4,128]{2,1,0:T(4,128)S(1)} %get-tuple-element.19), channel_id=1, source_target_pairs={{1,0},{2,1},{3,2},{4,3},{5,4},{6,5},{7,6},{0,7},{9,8},{10,9},{11,1... | collective-permute-start | bytes 196616 | tf_op jit(solution)/shard_map/ppermute | solution.py:219
  11.6 1.3 collective-permute-done
  12.9 4.5 %collective-permute-done.1 = f32[32,4,128]{2,1,0:T(4,128)S(1)} collective-permute-done((f32[32,4,128]{2,1,0:T(4,128)S(1)}, f32[32,4,128]{2,1,0:T(4,128)S(1)}, u32[]{:S(2)}, u32[]{:S(2)}) %collective-permute-start.1) | collective-permute-done | bytes 65568 | tf_op jit(solution)/shard_map/ppermute | solution.py:218
  18.0 4.0 %collective-permute-start.3 = (f32[4,136,128]{2,1,0:T(8,128)S(1)}, f32[4,136,128]{2,1,0:T(8,128)S(1)}, u32[]{:S(2)}, u32[]{:S(2)}) collective-permute-start(f32[4,136,128]{2,1,0:T(8,128)S(1)} %get-tuple-element.17), channel_id=1, source_target_pairs={{8,0},{16,8},{24,16},{9,1},{17,9},{25,17},{10,2},{18,10},{26,18},{... | collective-permute-start | bytes 835592 | tf_op jit(solution)/shard_map/ppermute | solution.py:219
  22.0 3.0 %collective-permute-start.2 = (f32[4,136,128]{2,1,0:T(8,128)S(1)}, f32[4,136,128]{2,1,0:T(8,128)S(1)}, u32[]{:S(2)}, u32[]{:S(2)}) collective-permute-start(f32[4,136,128]{2,1,0:T(8,128)S(1)} %get-tuple-element.18), channel_id=1, source_target_pairs={{0,8},{8,16},{16,24},{1,9},{9,17},{17,25},{2,10},{10,18},{18,26},{... | collective-permute-start | bytes 835592 | tf_op jit(solution)/shard_map/ppermute | solution.py:218
  25.9 12.9 %pack.1 = bf16[32,176,128]{2,1,0:T(8,128)(2,1)} custom-call(s32[4096]{0:T(1024)} %slot_ref.1, bf16[80,4096]{1,0:T(8,128)(2,1)} %weights_ref.1, f32[8,4096]{1,0:T(8,128)} %stack.31.extras_ref), custom_call_target="tpu_custom_call" | custom-call | bytes 31457280 | tf_op jit(solution)/shard_map/pack/pallas_call | solution.py:249
  39.6 2.4 %all-to-all-start = ((bf16[32,176,128]{2,1,0:T(8,128)(2,1)}), bf16[32,176,128]{2,1,0:T(8,128)(2,1)S(1)}, u32[]{:S(2)}, u32[]{:S(2)}) async-start(bf16[32,176,128]{2,1,0:T(8,128)(2,1)} %pack.1), calls=%async_computation | async-start | bytes 2883584 | tf_op jit(solution)/shard_map/all_to_all | solution.py:266
  42.0 2.9 %pad_maximum_fusion.field_ref = f32[40,136,128]{2,1,0:T(8,128)} fusion(f32[4,136,128]{2,1,0:T(8,128)} %copy-done.3, f32[32,4,128]{2,1,0:T(4,128)} %copy-done.6, f32[32,4,128]{2,1,0:T(4,128)} %copy-done.5, f32[32,128,128]{2,1,0:T(8,128)S(1)} %bitcast_add_fusion, f32[4,136,128]{2,1,0:T(8,128)} %copy-done.4), kind=kLoop, calls=%fused_computation | loop fusion | flops 2785280 | bytes 5570560 | tf_op jit(solution)/shard_map/concatenate | solution.py:267
  44.9 11.7 %forward.1 = (f32[32,128,128]{2,1,0:T(8,128)}, f32[40,136,128]{2,1,0:T(8,128)}) custom-call(f32[40,136,128]{2,1,0:T(8,128)} %pad_maximum_fusion.field_ref), custom_call_target="tpu_custom_call" | custom-call | flops 27852800 | bytes 8355840 | tf_op jit(solution)/shard_map/forward/pallas_call | solution.py:269
  56.6 20.2 %all-to-all-done.got_ref = bf16[32,176,128]{2,1,0:T(8,128)(2,1)S(1)} async-done(((bf16[32,176,128]{2,1,0:T(8,128)(2,1)}), bf16[32,176,128]{2,1,0:T(8,128)(2,1)S(1)}, u32[]{:S(2)}, u32[]{:S(2)}) %all-to-all-start) | async-done | bytes 1441824 | tf_op jit(solution)/shard_map/all_to_all | solution.py:266
  76.9 1.2 copy-done.1
  78.1 71.6 %observe.1 = f32[4096,128]{1,0:T(8,128)} custom-call(bf16[32,176,128]{2,1,0:T(8,128)(2,1)} %copy-done.1, f32[4096,128]{1,0:T(8,128)} %bitcast.21), custom_call_target="tpu_custom_call" | custom-call | tf_op jit(solution)/shard_map/observe/pallas_call | solution.py:283
  149.7 1.9 %convert.10 = bf16[32,128,128]{2,1,0:T(8,128)(2,1)S(1)} convert(f32[32,128,128]{2,1,0:T(8,128)} %bitcast.18) | non-fusion elementwise | flops 524288 | bytes 3145728 | tf_op jit(solution)/shard_map/convert.5
  151.7 1.0 collective-permute-start.4
  153.2 1.3 collective-permute-done.4
  154.5 3.6 %collective-permute-done.5 = bf16[32,4,128]{2,1,0:T(4,128)(2,1)S(1)} collective-permute-done((bf16[32,4,128]{2,1,0:T(4,128)(2,1)S(1)}, bf16[32,4,128]{2,1,0:T(4,128)(2,1)S(1)}, u32[]{:S(2)}, u32[]{:S(2)}) %collective-permute-start.5) | collective-permute-done | bytes 32800 | tf_op jit(solution)/shard_map/ppermute | solution.py:218
  158.2 4.3 %collective-permute-start.6 = (bf16[4,136,128]{2,1,0:T(8,128)(2,1)S(1)}, bf16[4,136,128]{2,1,0:T(8,128)(2,1)S(1)}, u32[]{:S(2)}, u32[]{:S(2)}) collective-permute-start(bf16[4,136,128]{2,1,0:T(8,128)(2,1)S(1)} %get-tuple-element.15), channel_id=1, source_target_pairs={{0,8},{8,16},{16,24},{1,9},{9,17},{17,25},{2,10},{10,18},{18,26},{... | collective-permute-start | bytes 417800 | tf_op jit(solution)/shard_map/ppermute | solution.py:218
  162.5 1.9 %collective-permute-start.7 = (bf16[4,136,128]{2,1,0:T(8,128)(2,1)S(1)}, bf16[4,136,128]{2,1,0:T(8,128)(2,1)S(1)}, u32[]{:S(2)}, u32[]{:S(2)}) collective-permute-start(bf16[4,136,128]{2,1,0:T(8,128)(2,1)S(1)} %get-tuple-element.16), channel_id=1, source_target_pairs={{8,0},{16,8},{24,16},{9,1},{17,9},{25,17},{10,2},{18,10},{26,18},{... | collective-permute-start | bytes 417800 | tf_op jit(solution)/shard_map/ppermute | solution.py:219
  164.5 4.3 %collective-permute-done.7 = bf16[4,136,128]{2,1,0:T(8,128)(2,1)S(1)} collective-permute-done((bf16[4,136,128]{2,1,0:T(8,128)(2,1)S(1)}, bf16[4,136,128]{2,1,0:T(8,128)(2,1)S(1)}, u32[]{:S(2)}, u32[]{:S(2)}) %collective-permute-start.7) | collective-permute-done | bytes 139296 | tf_op jit(solution)/shard_map/ppermute | solution.py:219
  168.9 1.8 pad_maximum_fusion.1.field_ref
  170.7 9.6 %adjoint.1 = f32[32,128,128]{2,1,0:T(8,128)} custom-call(f32[40,136,128]{2,1,0:T(8,128)} %pad_maximum_fusion.1.field_ref, f32[40,136,128]{2,1,0:T(8,128)} %get-tuple-element.14.kappa_ref), custom_call_target="tpu_custom_call" | custom-call | tf_op jit(solution)/shard_map/adjoint/pallas_call | solution.py:301
  180.2 4.6 %fusion.5 = f32[80,32,128]{2,0,1:T(8,128)S(1)} fusion(f32[32,128,128]{2,1,0:T(8,128)} %adjoint.1, f32[80,32,128]{2,1,0:T(8,128)S(1)} %copy-done.2, f32[80,80]{1,0:T(8,128)S(1)} %copy-done.7), kind=kOutput, calls=%fused_computation.6 | convolution fusion | flops 314900480 | bytes 4744192 | tf_op jit(solution)/shard_map/jk,abj->kab/dot_general | solution.py:310
  184.9 1.5 copy.14
  (41 shorter events, 3.9 us)
Async XLA Ops:
  6.4 18.7 %copy-start.9 = (bf16[4096]{0:T(1024)(128)(2,1)S(1)}, bf16[4096]{0:T(1024)(128)(2,1)}, u32[]{:S(2)}) copy-start(bf16[4096]{0:T(1024)(128)(2,1)} %param.12) | copy-start | bytes 24580
  6.4 18.7 %copy-start.10 = (bf16[4096]{0:T(1024)(128)(2,1)S(1)}, bf16[4096]{0:T(1024)(128)(2,1)}, u32[]{:S(2)}) copy-start(bf16[4096]{0:T(1024)(128)(2,1)} %param.13) | copy-start | bytes 24580
  6.4 18.7 %copy-start.8 = (s32[4096]{0:T(1024)S(1)}, s32[4096]{0:T(1024)}, u32[]{:S(2)}) copy-start(s32[4096]{0:T(1024)} %param.15) | copy-start | bytes 49156
  6.4 6.5 %collective-permute-start = (f32[32,4,128]{2,1,0:T(4,128)S(1)}, f32[32,4,128]{2,1,0:T(4,128)S(1)}, u32[]{:S(2)}, u32[]{:S(2)}) collective-permute-start(f32[32,4,128]{2,1,0:T(4,128)S(1)} %get-tuple-element.19), channel_id=1, source_target_pairs={{1,0},{2,1},{3,2},{4,3},{5,4},{6,5},{7,6},{0,7},{9,8},{10,9},{11,1... | collective-permute-start | bytes 196616 | tf_op jit(solution)/shard_map/ppermute | solution.py:219
  11.6 5.8 %collective-permute-start.1 = (f32[32,4,128]{2,1,0:T(4,128)S(1)}, f32[32,4,128]{2,1,0:T(4,128)S(1)}, u32[]{:S(2)}, u32[]{:S(2)}) collective-permute-start(f32[32,4,128]{2,1,0:T(4,128)S(1)} %get-tuple-element.20), channel_id=1, source_target_pairs={{0,1},{1,2},{2,3},{3,4},{4,5},{5,6},{6,7},{7,0},{8,9},{9,10},{10,1... | collective-permute-start | bytes 196616 | tf_op jit(solution)/shard_map/ppermute | solution.py:218
  12.9 4.5 %copy-start.5 = (f32[32,4,128]{2,1,0:T(4,128)}, f32[32,4,128]{2,1,0:T(4,128)S(1)}, u32[]{:S(2)}) copy-start(f32[32,4,128]{2,1,0:T(4,128)S(1)} %collective-permute-done) | copy-start | bytes 196612
  17.4 0.6 copy-start.6
  18.0 20.8 %collective-permute-start.3 = (f32[4,136,128]{2,1,0:T(8,128)S(1)}, f32[4,136,128]{2,1,0:T(8,128)S(1)}, u32[]{:S(2)}, u32[]{:S(2)}) collective-permute-start(f32[4,136,128]{2,1,0:T(8,128)S(1)} %get-tuple-element.17), channel_id=1, source_target_pairs={{8,0},{16,8},{24,16},{9,1},{17,9},{25,17},{10,2},{18,10},{26,18},{... | collective-permute-start | bytes 835592 | tf_op jit(solution)/shard_map/ppermute | solution.py:219
  22.0 16.8 %collective-permute-start.2 = (f32[4,136,128]{2,1,0:T(8,128)S(1)}, f32[4,136,128]{2,1,0:T(8,128)S(1)}, u32[]{:S(2)}, u32[]{:S(2)}) collective-permute-start(f32[4,136,128]{2,1,0:T(8,128)S(1)} %get-tuple-element.18), channel_id=1, source_target_pairs={{0,8},{8,16},{16,24},{1,9},{9,17},{17,25},{2,10},{10,18},{18,26},{... | collective-permute-start | bytes 835592 | tf_op jit(solution)/shard_map/ppermute | solution.py:218
  38.8 0.7 copy-start.3
  38.8 0.8 copy-start.4
  39.6 37.3 %all-to-all-start = ((bf16[32,176,128]{2,1,0:T(8,128)(2,1)}), bf16[32,176,128]{2,1,0:T(8,128)(2,1)S(1)}, u32[]{:S(2)}, u32[]{:S(2)}) async-start(bf16[32,176,128]{2,1,0:T(8,128)(2,1)} %pack.1), calls=%async_computation | async-start | bytes 2883584 | tf_op jit(solution)/shard_map/all_to_all | solution.py:266
  76.9 1.2 copy-start.1
  149.7 8.4 %copy-start = (f32[4096,128]{1,0:T(8,128)S(1)}, f32[4096,128]{1,0:T(8,128)}, u32[]{:S(2)}) copy-start(f32[4096,128]{1,0:T(8,128)} %observe.1) | copy-start | bytes 6291460
  151.7 2.8 %collective-permute-start.4 = (bf16[32,4,128]{2,1,0:T(4,128)(2,1)S(1)}, bf16[32,4,128]{2,1,0:T(4,128)(2,1)S(1)}, u32[]{:S(2)}, u32[]{:S(2)}) collective-permute-start(bf16[32,4,128]{2,1,0:T(4,128)(2,1)S(1)} %get-tuple-element.21), channel_id=1, source_target_pairs={{1,0},{2,1},{3,2},{4,3},{5,4},{6,5},{7,6},{0,7},{9,8},{10,9},{11,1... | collective-permute-start | bytes 98312 | tf_op jit(solution)/shard_map/ppermute | solution.py:219
  152.6 5.5 %collective-permute-start.5 = (bf16[32,4,128]{2,1,0:T(4,128)(2,1)S(1)}, bf16[32,4,128]{2,1,0:T(4,128)(2,1)S(1)}, u32[]{:S(2)}, u32[]{:S(2)}) collective-permute-start(bf16[32,4,128]{2,1,0:T(4,128)(2,1)S(1)} %get-tuple-element.22), channel_id=1, source_target_pairs={{0,1},{1,2},{2,3},{3,4},{4,5},{5,6},{6,7},{7,0},{8,9},{9,10},{10,1... | collective-permute-start | bytes 98312 | tf_op jit(solution)/shard_map/ppermute | solution.py:218
  158.2 6.3 %collective-permute-start.6 = (bf16[4,136,128]{2,1,0:T(8,128)(2,1)S(1)}, bf16[4,136,128]{2,1,0:T(8,128)(2,1)S(1)}, u32[]{:S(2)}, u32[]{:S(2)}) collective-permute-start(bf16[4,136,128]{2,1,0:T(8,128)(2,1)S(1)} %get-tuple-element.15), channel_id=1, source_target_pairs={{0,8},{8,16},{16,24},{1,9},{9,17},{17,25},{2,10},{10,18},{18,26},{... | collective-permute-start | bytes 417800 | tf_op jit(solution)/shard_map/ppermute | solution.py:218
  162.5 6.4 %collective-permute-start.7 = (bf16[4,136,128]{2,1,0:T(8,128)(2,1)S(1)}, bf16[4,136,128]{2,1,0:T(8,128)(2,1)S(1)}, u32[]{:S(2)}, u32[]{:S(2)}) collective-permute-start(bf16[4,136,128]{2,1,0:T(8,128)(2,1)S(1)} %get-tuple-element.16), channel_id=1, source_target_pairs={{8,0},{16,8},{24,16},{9,1},{17,9},{25,17},{10,2},{18,10},{26,18},{... | collective-permute-start | bytes 417800 | tf_op jit(solution)/shard_map/ppermute | solution.py:219
  170.7 9.6 %copy-start.2 = (f32[80,32,128]{2,1,0:T(8,128)S(1)}, f32[80,32,128]{2,1,0:T(8,128)}, u32[]{:S(2)}) copy-start(f32[80,32,128]{2,1,0:T(8,128)} %param.8) | copy-start | bytes 3932164
  170.7 9.6 %copy-start.7 = (f32[80,80]{1,0:T(8,128)S(1)}, f32[80,80]{1,0:T(8,128)}, u32[]{:S(2)}) copy-start(f32[80,80]{1,0:T(8,128)} %param.9) | copy-start | bytes 76804

commit v3 on v2

--- a/solution.py
+++ b/solution.py
@@ -75,12 +75,10 @@
         out_ref[o, half:, :] = tails.astype(jnp.bfloat16)
 
 
-def obs_kernel(levels, lon_cells, got_ref, state_ref, out_ref, picked, weights, cols, col_ref, sem, *sums):
-    cells = state_ref.shape[0]
+def unpack_kernel(levels, lon_cells, got_ref, weights, cols):
     owners, slot_count = cols.shape
     half = slot_count // 2
     tail, beside, group = packing(levels, slot_count)
-    unroll = min(slot_count, 32)
     lane = lax.broadcasted_iota(jnp.int32, (8, LANES), 1)
     scale = jnp.where(lane == levels + 2, float(lon_cells), jnp.where(lane == levels + 3, 1.0, 0.0))
     scale = scale.astype(jnp.bfloat16)
@@ -105,8 +103,10 @@
         )
         cols[pl.ds(o, 1), :] = column[:1].astype(jnp.int32)
 
-    copy = pltpu.make_async_copy(cols, col_ref, sem)
-    copy.start()
+
+def obs_kernel(levels, col_ref, got_ref, state_ref, out_ref, picked, *sums):
+    count = picked.shape[0]
+    cells = state_ref.shape[0]
 
     @pl.loop(0, cells // 256)
     def _(j):
@@ -114,34 +114,28 @@
         for s in sums:
             s[pl.ds(at, 256), :] = jnp.zeros((256, LANES), jnp.float32)
 
-    copy.wait()
-
-    @pl.loop(0, owners)
-    def _(o):
-        @pl.loop(0, slot_count // unroll)
-        def _(j):
-            at = pl.multiple_of(o * slot_count + j * unroll, unroll)
-            for u in range(unroll):
-                picked[pl.ds(at + u, 1), :] = state_ref[pl.ds(col_ref[o, j * unroll + u], 1), :]
-
-    @pl.loop(0, owners * slot_count // 128)
+    @pl.loop(0, count // 32)
+    def _(j):
+        at = pl.multiple_of(j * 32, 32)
+        for u in range(32):
+            picked[pl.ds(at + u, 1), :] = state_ref[pl.ds(col_ref[at + u], 1), :]
+
+    @pl.loop(0, count // 128)
     def _(j):
         at = pl.multiple_of(j * 128, 128)
-        w = weights[pl.ds(at, 128), :]
+        w = got_ref[pl.ds(at, 128), :].astype(jnp.float32)
         model = jnp.sum(w * picked[pl.ds(at, 128), :], axis=1, keepdims=True)
         weighted = w[:, levels + 1 : levels + 2] * (model - w[:, levels : levels + 1])
         picked[pl.ds(at, 128), :] = w * weighted
 
-    @pl.loop(0, owners)
-    def _(o):
-        @pl.loop(0, slot_count // unroll)
-        def _(j):
-            at = pl.multiple_of(o * slot_count + j * unroll, unroll)
-            for u in range(0, unroll, CHAINS):
-                where = [col_ref[o, j * unroll + u + c] for c in range(CHAINS)]
-                old = [sums[c][pl.ds(where[c], 1), :] for c in range(CHAINS)]
-                for c in range(CHAINS):
-                    sums[c][pl.ds(where[c], 1), :] = old[c] + picked[pl.ds(at + u + c, 1), :]
+    @pl.loop(0, count // 32)
+    def _(j):
+        at = pl.multiple_of(j * 32, 32)
+        for u in range(0, 32, CHAINS):
+            cols = [col_ref[at + u + c] for c in range(CHAINS)]
+            old = [sums[c][pl.ds(cols[c], 1), :] for c in range(CHAINS)]
+            for c in range(CHAINS):
+                sums[c][pl.ds(cols[c], 1), :] = old[c] + picked[pl.ds(at + u + c, 1), :]
 
     @pl.loop(0, cells // 64)
     def _(j):
@@ -280,22 +274,26 @@
         name="forward",
     )(start)
 
+    got, columns = pl.pallas_call(
+        functools.partial(unpack_kernel, levels, lon_cells),
+        out_shape=(
+            jax.ShapeDtypeStruct((total, LANES), f32),
+            jax.ShapeDtypeStruct((devices, slot_count), jnp.int32),
+        ),
+        in_specs=[VMEM],
+        out_specs=(VMEM, VMEM),
+        compiler_params=PARAMS,
+        name="unpack",
+    )(got)
     adjoint = pl.pallas_call(
-        functools.partial(obs_kernel, levels, lon_cells),
+        functools.partial(obs_kernel, levels),
         out_shape=jax.ShapeDtypeStruct((cells, LANES), f32),
-        in_specs=[VMEM, VMEM],
+        in_specs=[SMEM, VMEM, VMEM],
         out_specs=VMEM,
-        scratch_shapes=[
-            pltpu.VMEM((total, LANES), f32),
-            pltpu.VMEM((total, LANES), f32),
-            pltpu.VMEM((devices, slot_count), jnp.int32),
-            pltpu.SMEM((devices, slot_count), jnp.int32),
-            pltpu.SemaphoreType.DMA,
-        ]
-        + [pltpu.VMEM((cells, LANES), f32)] * CHAINS,
+        scratch_shapes=[pltpu.VMEM((total, LANES), f32)] + [pltpu.VMEM((cells, LANES), f32)] * CHAINS,
         compiler_params=PARAMS,
         name="observe",
-    )(got, state.reshape(cells, LANES))
+    )(columns.reshape(total), got, state.reshape(cells, LANES))
 
     adjoint = extended(adjoint.reshape(lat_rows, lon_cells, LANES), jnp.bfloat16)
     adjoint = pl.pallas_call(

time: 187 us -> 165 us (0.88)
  Pallas kernels: 106 us -> 82.9 us
    pallas_call x1 -> x2, Pallas kernels: 71.6 us -> 48.7 us  [the longest x1 38.1 us: local(): pl.pallas_call(functools.partial(obs_kernel, levels), out_shape=jax.Shape...]
    unnamed x23 -> x24, local copies, waits for them, and re-layouts: 3.43 us -> 4.74 us
  transfers between devices with their start and end apart: 9 -> 9, of which waited for: 7 -> 6; matrix products, arithmetic and copies ran while one was open for 2% -> 2% of each run, Pallas kernels for 13% -> 15%
where the time goes in v3:
time: 165 us
  Pallas kernels  82.9 us (50%)
  waiting for transfers between devices  35 us (21%)
  starting transfers between devices  22.7 us (14%)
  matrix products  10.1 us (6%)
  local copies, waits for them, and re-layouts  7.04 us (4%)
  other arithmetic  6.7 us (4%)
    pallas_call x1, Pallas kernels, local(): pl.pallas_call(functools.partial(obs_kernel, levels), out_shape=jax.Shape...  38.1 us
    all_to_all x1, waiting for transfers between devices, local(): lax.all_to_all(send, ('lat', 'lon'), split_axis=0, concat_axis=0, tiled=T...  20.2 us
    pallas_call x1, Pallas kernels, local(): pl.pallas_call(pack_kernel, out_shape=jax.ShapeDtypeStruct((devices, pack...  12.8 us
    ppermute x4, starting transfers between devices, exchange(): high = lax.ppermute(high, axis, backward).astype(block.dtype)  12.4 us
    pallas_call x1, Pallas kernels, local(): pl.pallas_call(functools.partial(forward_kernel, levels), out_shape=(jax....  11.8 us
    pallas_call x1, Pallas kernels, local(): pl.pallas_call(functools.partial(unpack_kernel, levels, lon_cells), out_s...  10.6 us
    pallas_call x1, Pallas kernels, local(): pl.pallas_call(adjoint_kernel, out_shape=jax.ShapeDtypeStruct((lat_rows,...  9.63 us
    ppermute x4, waiting for transfers between devices, exchange(): low = lax.ppermute(low, axis, forward).astype(block.dtype)  8.07 us
  transfers between devices with their start and end apart: 9, of which 6 were waited for; matrix products, arithmetic and copies ran while one was open for 2% of the time, Pallas kernels for 15%

profile of v3, /device:TPU:1, one launch (start us, length us, event | category | flops | bytes accessed | tf_op | source)
XLA Modules:
  0.0 164.7 jit_solution(266863468967745394)
XLA Ops:
  0.9 5.5 %bitcast_add_fusion = f32[32,128,128]{2,1,0:T(8,128)S(1)} fusion(f32[80,32,128]{2,1,0:T(8,128)} %param.8, f32[128]{0:T(128)S(1)} %compare_convert_fusion, f32[32,128]{1,0:T(8,128)} %param.10, f32[80,80]{0,1:T(8,128)S(1)} %copy.9), kind=kOutput, calls=%fused_computation.4 | convolution fusion | flops 504365056 | bytes 3450368 | tf_op jit(solution)/shard_map/kj,jab->abk/dot_general | solution.py:254
  6.4 5.2 %collective-permute-start = (f32[32,4,128]{2,1,0:T(4,128)S(1)}, f32[32,4,128]{2,1,0:T(4,128)S(1)}, u32[]{:S(2)}, u32[]{:S(2)}) collective-permute-start(f32[32,4,128]{2,1,0:T(4,128)S(1)} %get-tuple-element.23), channel_id=1, source_target_pairs={{1,0},{2,1},{3,2},{4,3},{5,4},{6,5},{7,6},{0,7},{9,8},{10,9},{11,1... | collective-permute-start | bytes 196616 | tf_op jit(solution)/shard_map/ppermute | solution.py:213
  11.6 1.3 collective-permute-done
  12.9 4.5 %collective-permute-done.1 = f32[32,4,128]{2,1,0:T(4,128)S(1)} collective-permute-done((f32[32,4,128]{2,1,0:T(4,128)S(1)}, f32[32,4,128]{2,1,0:T(4,128)S(1)}, u32[]{:S(2)}, u32[]{:S(2)}) %collective-permute-start.1) | collective-permute-done | bytes 65568 | tf_op jit(solution)/shard_map/ppermute | solution.py:212
  18.0 4.0 %collective-permute-start.3 = (f32[4,136,128]{2,1,0:T(8,128)S(1)}, f32[4,136,128]{2,1,0:T(8,128)S(1)}, u32[]{:S(2)}, u32[]{:S(2)}) collective-permute-start(f32[4,136,128]{2,1,0:T(8,128)S(1)} %get-tuple-element.21), channel_id=1, source_target_pairs={{8,0},{16,8},{24,16},{9,1},{17,9},{25,17},{10,2},{18,10},{26,18},{... | collective-permute-start | bytes 835592 | tf_op jit(solution)/shard_map/ppermute | solution.py:213
  22.0 3.0 %collective-permute-start.2 = (f32[4,136,128]{2,1,0:T(8,128)S(1)}, f32[4,136,128]{2,1,0:T(8,128)S(1)}, u32[]{:S(2)}, u32[]{:S(2)}) collective-permute-start(f32[4,136,128]{2,1,0:T(8,128)S(1)} %get-tuple-element.22), channel_id=1, source_target_pairs={{0,8},{8,16},{16,24},{1,9},{9,17},{17,25},{2,10},{10,18},{18,26},{... | collective-permute-start | bytes 835592 | tf_op jit(solution)/shard_map/ppermute | solution.py:212
  25.9 12.8 %pack.1 = bf16[32,176,128]{2,1,0:T(8,128)(2,1)} custom-call(s32[4096]{0:T(1024)} %slot_ref.1, bf16[80,4096]{1,0:T(8,128)(2,1)} %weights_ref.1, f32[8,4096]{1,0:T(8,128)} %stack.31.extras_ref), custom_call_target="tpu_custom_call" | custom-call | bytes 31457280 | tf_op jit(solution)/shard_map/pack/pallas_call | solution.py:243
  39.5 2.4 %all-to-all-start = ((bf16[32,176,128]{2,1,0:T(8,128)(2,1)}), bf16[32,176,128]{2,1,0:T(8,128)(2,1)S(1)}, u32[]{:S(2)}, u32[]{:S(2)}) async-start(bf16[32,176,128]{2,1,0:T(8,128)(2,1)} %pack.1), calls=%async_computation | async-start | bytes 2883584 | tf_op jit(solution)/shard_map/all_to_all | solution.py:260
  42.0 2.9 %pad_maximum_fusion.field_ref = f32[40,136,128]{2,1,0:T(8,128)} fusion(f32[4,136,128]{2,1,0:T(8,128)} %copy-done.3, f32[32,4,128]{2,1,0:T(4,128)} %copy-done.6, f32[32,4,128]{2,1,0:T(4,128)} %copy-done.5, f32[32,128,128]{2,1,0:T(8,128)S(1)} %bitcast_add_fusion, f32[4,136,128]{2,1,0:T(8,128)} %copy-done.4), kind=kLoop, calls=%fused_computation | loop fusion | flops 2785280 | bytes 5570560 | tf_op jit(solution)/shard_map/concatenate | solution.py:261
  44.8 11.8 %forward.1 = (f32[32,128,128]{2,1,0:T(8,128)}, f32[40,136,128]{2,1,0:T(8,128)}) custom-call(f32[40,136,128]{2,1,0:T(8,128)} %pad_maximum_fusion.field_ref), custom_call_target="tpu_custom_call" | custom-call | flops 27852800 | bytes 8355840 | tf_op jit(solution)/shard_map/forward/pallas_call | solution.py:263
  56.6 20.2 %all-to-all-done.got_ref = bf16[32,176,128]{2,1,0:T(8,128)(2,1)S(1)} async-done(((bf16[32,176,128]{2,1,0:T(8,128)(2,1)}), bf16[32,176,128]{2,1,0:T(8,128)(2,1)S(1)}, u32[]{:S(2)}, u32[]{:S(2)}) %all-to-all-start) | async-done | bytes 1441824 | tf_op jit(solution)/shard_map/all_to_all | solution.py:260
  77.9 10.6 %unpack.1 = (f32[8192,128]{1,0:T(8,128)}, s32[32,256]{1,0:T(8,128)}) custom-call(bf16[32,176,128]{2,1,0:T(8,128)(2,1)} %copy-done.1), custom_call_target="tpu_custom_call" | custom-call | tf_op jit(solution)/shard_map/unpack/pallas_call | solution.py:277
  88.5 1.4 copy.18
  89.9 38.1 %observe.1 = f32[4096,128]{1,0:T(8,128)} custom-call(s32[8192]{0:T(1024)} %bitcast.24, f32[8192,128]{1,0:T(8,128)} %get-tuple-element.14.got_ref, f32[4096,128]{1,0:T(8,128)} %bitcast.23), custom_call_target="tpu_custom_call" | custom-call | tf_op jit(solution)/shard_map/observe/pallas_call | solution.py:288
  128.0 1.9 %convert.10 = bf16[32,128,128]{2,1,0:T(8,128)(2,1)S(1)} convert(f32[32,128,128]{2,1,0:T(8,128)} %bitcast.20) | non-fusion elementwise | flops 524288 | bytes 3145728 | tf_op jit(solution)/shard_map/convert.5
  131.5 1.3 collective-permute-done.4
  132.8 3.6 %collective-permute-done.5 = bf16[32,4,128]{2,1,0:T(4,128)(2,1)S(1)} collective-permute-done((bf16[32,4,128]{2,1,0:T(4,128)(2,1)S(1)}, bf16[32,4,128]{2,1,0:T(4,128)(2,1)S(1)}, u32[]{:S(2)}, u32[]{:S(2)}) %collective-permute-start.5) | collective-permute-done | bytes 32800 | tf_op jit(solution)/shard_map/ppermute | solution.py:212
  136.5 4.3 %collective-permute-start.6 = (bf16[4,136,128]{2,1,0:T(8,128)(2,1)S(1)}, bf16[4,136,128]{2,1,0:T(8,128)(2,1)S(1)}, u32[]{:S(2)}, u32[]{:S(2)}) collective-permute-start(bf16[4,136,128]{2,1,0:T(8,128)(2,1)S(1)} %get-tuple-element.19), channel_id=1, source_target_pairs={{0,8},{8,16},{16,24},{1,9},{9,17},{17,25},{2,10},{10,18},{18,26},{... | collective-permute-start | bytes 417800 | tf_op jit(solution)/shard_map/ppermute | solution.py:212
  140.8 2.3 %collective-permute-start.7 = (bf16[4,136,128]{2,1,0:T(8,128)(2,1)S(1)}, bf16[4,136,128]{2,1,0:T(8,128)(2,1)S(1)}, u32[]{:S(2)}, u32[]{:S(2)}) collective-permute-start(bf16[4,136,128]{2,1,0:T(8,128)(2,1)S(1)} %get-tuple-element.20), channel_id=1, source_target_pairs={{8,0},{16,8},{24,16},{9,1},{17,9},{25,17},{10,2},{18,10},{26,18},{... | collective-permute-start | bytes 417800 | tf_op jit(solution)/shard_map/ppermute | solution.py:213
  143.1 4.1 %collective-permute-done.7 = bf16[4,136,128]{2,1,0:T(8,128)(2,1)S(1)} collective-permute-done((bf16[4,136,128]{2,1,0:T(8,128)(2,1)S(1)}, bf16[4,136,128]{2,1,0:T(8,128)(2,1)S(1)}, u32[]{:S(2)}, u32[]{:S(2)}) %collective-permute-start.7) | collective-permute-done | bytes 139296 | tf_op jit(solution)/shard_map/ppermute | solution.py:213
  147.2 1.8 %pad_maximum_fusion.1.field_ref = f32[40,136,128]{2,1,0:T(8,128)} fusion(f32[4,136,128]{2,1,0:T(8,128)S(1)} %convert_element_type.39, f32[32,4,128]{2,1,0:T(4,128)S(1)} %convert_element_type.37, f32[32,4,128]{2,1,0:T(4,128)S(1)} %convert_element_type.36, f32[32,128,128]{2,1,0:T(8,128)S(1)} %bitcast.22, f32[4,136,128]{2,1,0:T(8,128)S(1)} %convert_element_type.38), kind=kLoop, calls=%fused_computation.1 | loop fusion | flops 2785280 | bytes 5570560 | tf_op jit(solution)/shard_map/concatenate | solution.py:221
  148.9 9.6 %adjoint.1 = f32[32,128,128]{2,1,0:T(8,128)} custom-call(f32[40,136,128]{2,1,0:T(8,128)} %pad_maximum_fusion.1.field_ref, f32[40,136,128]{2,1,0:T(8,128)} %get-tuple-element.18.kappa_ref), custom_call_target="tpu_custom_call" | custom-call | tf_op jit(solution)/shard_map/adjoint/pallas_call | solution.py:299
  158.6 4.6 %fusion.5 = f32[80,32,128]{2,0,1:T(8,128)S(1)} fusion(f32[32,128,128]{2,1,0:T(8,128)} %adjoint.1, f32[80,32,128]{2,1,0:T(8,128)S(1)} %copy-done.2, f32[80,80]{1,0:T(8,128)S(1)} %copy-done.7), kind=kOutput, calls=%fused_computation.6 | convolution fusion | flops 314900480 | bytes 4744192 | tf_op jit(solution)/shard_map/jk,abj->kab/dot_general | solution.py:308
  163.2 1.5 copy.14
  (43 shorter events, 5.9 us)
Async XLA Ops:
  6.4 18.7 %copy-start.9 = (bf16[4096]{0:T(1024)(128)(2,1)S(1)}, bf16[4096]{0:T(1024)(128)(2,1)}, u32[]{:S(2)}) copy-start(bf16[4096]{0:T(1024)(128)(2,1)} %param.12) | copy-start | bytes 24580
  6.4 18.7 %copy-start.10 = (bf16[4096]{0:T(1024)(128)(2,1)S(1)}, bf16[4096]{0:T(1024)(128)(2,1)}, u32[]{:S(2)}) copy-start(bf16[4096]{0:T(1024)(128)(2,1)} %param.13) | copy-start | bytes 24580
  6.4 18.7 %copy-start.8 = (s32[4096]{0:T(1024)S(1)}, s32[4096]{0:T(1024)}, u32[]{:S(2)}) copy-start(s32[4096]{0:T(1024)} %param.15) | copy-start | bytes 49156
  6.4 6.5 %collective-permute-start = (f32[32,4,128]{2,1,0:T(4,128)S(1)}, f32[32,4,128]{2,1,0:T(4,128)S(1)}, u32[]{:S(2)}, u32[]{:S(2)}) collective-permute-start(f32[32,4,128]{2,1,0:T(4,128)S(1)} %get-tuple-element.23), channel_id=1, source_target_pairs={{1,0},{2,1},{3,2},{4,3},{5,4},{6,5},{7,6},{0,7},{9,8},{10,9},{11,1... | collective-permute-start | bytes 196616 | tf_op jit(solution)/shard_map/ppermute | solution.py:213
  11.6 5.8 %collective-permute-start.1 = (f32[32,4,128]{2,1,0:T(4,128)S(1)}, f32[32,4,128]{2,1,0:T(4,128)S(1)}, u32[]{:S(2)}, u32[]{:S(2)}) collective-permute-start(f32[32,4,128]{2,1,0:T(4,128)S(1)} %get-tuple-element.24), channel_id=1, source_target_pairs={{0,1},{1,2},{2,3},{3,4},{4,5},{5,6},{6,7},{7,0},{8,9},{9,10},{10,1... | collective-permute-start | bytes 196616 | tf_op jit(solution)/shard_map/ppermute | solution.py:212
  12.9 4.5 %copy-start.5 = (f32[32,4,128]{2,1,0:T(4,128)}, f32[32,4,128]{2,1,0:T(4,128)S(1)}, u32[]{:S(2)}) copy-start(f32[32,4,128]{2,1,0:T(4,128)S(1)} %collective-permute-done) | copy-start | bytes 196612
  17.4 0.6 copy-start.6
  18.0 20.7 %collective-permute-start.3 = (f32[4,136,128]{2,1,0:T(8,128)S(1)}, f32[4,136,128]{2,1,0:T(8,128)S(1)}, u32[]{:S(2)}, u32[]{:S(2)}) collective-permute-start(f32[4,136,128]{2,1,0:T(8,128)S(1)} %get-tuple-element.21), channel_id=1, source_target_pairs={{8,0},{16,8},{24,16},{9,1},{17,9},{25,17},{10,2},{18,10},{26,18},{... | collective-permute-start | bytes 835592 | tf_op jit(solution)/shard_map/ppermute | solution.py:213
  22.0 16.7 %collective-permute-start.2 = (f32[4,136,128]{2,1,0:T(8,128)S(1)}, f32[4,136,128]{2,1,0:T(8,128)S(1)}, u32[]{:S(2)}, u32[]{:S(2)}) collective-permute-start(f32[4,136,128]{2,1,0:T(8,128)S(1)} %get-tuple-element.22), channel_id=1, source_target_pairs={{0,8},{8,16},{16,24},{1,9},{9,17},{17,25},{2,10},{10,18},{18,26},{... | collective-permute-start | bytes 835592 | tf_op jit(solution)/shard_map/ppermute | solution.py:212
  38.7 0.7 copy-start.3
  38.8 0.8 copy-start.4
  39.5 37.3 %all-to-all-start = ((bf16[32,176,128]{2,1,0:T(8,128)(2,1)}), bf16[32,176,128]{2,1,0:T(8,128)(2,1)S(1)}, u32[]{:S(2)}, u32[]{:S(2)}) async-start(bf16[32,176,128]{2,1,0:T(8,128)(2,1)} %pack.1), calls=%async_computation | async-start | bytes 2883584 | tf_op jit(solution)/shard_map/all_to_all | solution.py:260
  76.8 1.1 copy-start.1
  128.0 8.4 %copy-start = (f32[4096,128]{1,0:T(8,128)S(1)}, f32[4096,128]{1,0:T(8,128)}, u32[]{:S(2)}) copy-start(f32[4096,128]{1,0:T(8,128)} %observe.1) | copy-start | bytes 6291460
  130.0 2.8 %collective-permute-start.4 = (bf16[32,4,128]{2,1,0:T(4,128)(2,1)S(1)}, bf16[32,4,128]{2,1,0:T(4,128)(2,1)S(1)}, u32[]{:S(2)}, u32[]{:S(2)}) collective-permute-start(bf16[32,4,128]{2,1,0:T(4,128)(2,1)S(1)} %get-tuple-element.25), channel_id=1, source_target_pairs={{1,0},{2,1},{3,2},{4,3},{5,4},{6,5},{7,6},{0,7},{9,8},{10,9},{11,1... | collective-permute-start | bytes 98312 | tf_op jit(solution)/shard_map/ppermute | solution.py:213
  130.9 5.5 %collective-permute-start.5 = (bf16[32,4,128]{2,1,0:T(4,128)(2,1)S(1)}, bf16[32,4,128]{2,1,0:T(4,128)(2,1)S(1)}, u32[]{:S(2)}, u32[]{:S(2)}) collective-permute-start(bf16[32,4,128]{2,1,0:T(4,128)(2,1)S(1)} %get-tuple-element.26), channel_id=1, source_target_pairs={{0,1},{1,2},{2,3},{3,4},{4,5},{5,6},{6,7},{7,0},{8,9},{9,10},{10,1... | collective-permute-start | bytes 98312 | tf_op jit(solution)/shard_map/ppermute | solution.py:212
  136.5 6.6 %collective-permute-start.6 = (bf16[4,136,128]{2,1,0:T(8,128)(2,1)S(1)}, bf16[4,136,128]{2,1,0:T(8,128)(2,1)S(1)}, u32[]{:S(2)}, u32[]{:S(2)}) collective-permute-start(bf16[4,136,128]{2,1,0:T(8,128)(2,1)S(1)} %get-tuple-element.19), channel_id=1, source_target_pairs={{0,8},{8,16},{16,24},{1,9},{9,17},{17,25},{2,10},{10,18},{18,26},{... | collective-permute-start | bytes 417800 | tf_op jit(solution)/shard_map/ppermute | solution.py:212
  140.8 6.4 %collective-permute-start.7 = (bf16[4,136,128]{2,1,0:T(8,128)(2,1)S(1)}, bf16[4,136,128]{2,1,0:T(8,128)(2,1)S(1)}, u32[]{:S(2)}, u32[]{:S(2)}) collective-permute-start(bf16[4,136,128]{2,1,0:T(8,128)(2,1)S(1)} %get-tuple-element.20), channel_id=1, source_target_pairs={{8,0},{16,8},{24,16},{9,1},{17,9},{25,17},{10,2},{18,10},{26,18},{... | collective-permute-start | bytes 417800 | tf_op jit(solution)/shard_map/ppermute | solution.py:213
  148.9 9.6 %copy-start.2 = (f32[80,32,128]{2,1,0:T(8,128)S(1)}, f32[80,32,128]{2,1,0:T(8,128)}, u32[]{:S(2)}) copy-start(f32[80,32,128]{2,1,0:T(8,128)} %param.8) | copy-start | bytes 3932164
  148.9 9.6 %copy-start.7 = (f32[80,80]{1,0:T(8,128)S(1)}, f32[80,80]{1,0:T(8,128)}, u32[]{:S(2)}) copy-start(f32[80,80]{1,0:T(8,128)} %param.9) | copy-start | bytes 76804

commit v4 on v3

--- a/solution.py
+++ b/solution.py
@@ -28,7 +28,7 @@
     obs = rows.shape[0]
     rest = LANES - weights_ref.shape[0] - extras_ref.shape[0]
 
-    @pl.loop(0, obs // LANES)
+    @pl.loop(0, obs // LANES, unroll=4)
     def _(j):
         at = pl.multiple_of(j * LANES, LANES)
         block = [
@@ -56,7 +56,7 @@
     head_lane = lax.broadcasted_iota(jnp.int32, (half, LANES), 1)
     tail_lane = lax.broadcasted_iota(jnp.int32, (group, LANES), 1)
 
-    @pl.loop(0, owners)
+    @pl.loop(0, owners, unroll=4)
     def _(o):
         at = pl.multiple_of(o * count, count)
         second = pltpu.roll(slots[pl.ds(at + half, half), :], HEAD, 1)
@@ -83,7 +83,7 @@
     scale = jnp.where(lane == levels + 2, float(lon_cells), jnp.where(lane == levels + 3, 1.0, 0.0))
     scale = scale.astype(jnp.bfloat16)
 
-    @pl.loop(0, owners)
+    @pl.loop(0, owners, unroll=4)
     def _(o):
         at = pl.multiple_of(o * slot_count, slot_count)
         head = got_ref[o, :half, :].astype(jnp.float32)
@@ -120,7 +120,7 @@
         for u in range(32):
             picked[pl.ds(at + u, 1), :] = state_ref[pl.ds(col_ref[at + u], 1), :]
 
-    @pl.loop(0, count // 128)
+    @pl.loop(0, count // 128, unroll=4)
     def _(j):
         at = pl.multiple_of(j * 128, 128)
         w = got_ref[pl.ds(at, 128), :].astype(jnp.float32)

time: 165 us -> 149 us (0.903)
  Pallas kernels: 82.9 us -> 65.6 us
    pallas_call x1, Pallas kernels: 38.1 us -> 29.7 us  [local(): pl.pallas_call(functools.partial(obs_kernel, levels), out_shape=jax.Shape...]
    pallas_call x1, Pallas kernels: 10.6 us -> 5.61 us  [local(): pl.pallas_call(functools.partial(unpack_kernel, levels, lon_cells), out_s...]
    pallas_call x1, Pallas kernels: 12.8 us -> 8.87 us  [local(): pl.pallas_call(pack_kernel, out_shape=jax.ShapeDtypeStruct((devices, pack...]
    ppermute x4, starting transfers between devices: 7.89 us -> 6.19 us  [exchange(): low = lax.ppermute(low, axis, forward).astype(block.dtype)]
  transfers between devices with their start and end apart: 9 -> 9, of which waited for: 6 -> 7; matrix products, arithmetic and copies ran while one was open for 2% -> 3% of each run, Pallas kernels for 15% -> 14%
where the time goes in v4:
time: 149 us; the launch traced here: 148 us
  Pallas kernels  65.6 us (44%)
  waiting for transfers between devices  35.9 us (24%)
  starting transfers between devices  22.1 us (15%)
  matrix products  10.1 us (7%)
  local copies, waits for them, and re-layouts  7.04 us (5%)
  other arithmetic  6.7 us (4%)
    pallas_call x1, Pallas kernels, local(): pl.pallas_call(functools.partial(obs_kernel, levels), out_shape=jax.Shape...  29.7 us
    all_to_all x1, waiting for transfers between devices, local(): lax.all_to_all(send, ('lat', 'lon'), split_axis=0, concat_axis=0, tiled=T...  20.2 us
    ppermute x4, starting transfers between devices, exchange(): high = lax.ppermute(high, axis, backward).astype(block.dtype)  13.5 us
    pallas_call x1, Pallas kernels, local(): pl.pallas_call(functools.partial(forward_kernel, levels), out_shape=(jax....  11.8 us
    pallas_call x1, Pallas kernels, local(): pl.pallas_call(adjoint_kernel, out_shape=jax.ShapeDtypeStruct((lat_rows,...  9.63 us
    ppermute x4, waiting for transfers between devices, exchange(): low = lax.ppermute(low, axis, forward).astype(block.dtype)  8.91 us
    pallas_call x1, Pallas kernels, local(): pl.pallas_call(pack_kernel, out_shape=jax.ShapeDtypeStruct((devices, pack...  8.87 us
    ppermute x4, waiting for transfers between devices, exchange(): high = lax.ppermute(high, axis, backward).astype(block.dtype)  6.77 us
  transfers between devices with their start and end apart: 9, of which 7 were waited for; matrix products, arithmetic and copies ran while one was open for 3% of the time, Pallas kernels for 14%

profile of v4, /device:TPU:1, one launch (start us, length us, event | category | flops | bytes accessed | tf_op | source)
XLA Modules:
  0.0 147.7 jit_solution(4661854121218195923)
XLA Ops:
  0.9 5.5 %bitcast_add_fusion = f32[32,128,128]{2,1,0:T(8,128)S(1)} fusion(f32[80,32,128]{2,1,0:T(8,128)} %param.8, f32[128]{0:T(128)S(1)} %compare_convert_fusion, f32[32,128]{1,0:T(8,128)} %param.10, f32[80,80]{0,1:T(8,128)S(1)} %copy.9), kind=kOutput, calls=%fused_computation.4 | convolution fusion | flops 504365056 | bytes 3450368 | tf_op jit(solution)/shard_map/kj,jab->abk/dot_general | solution.py:254
  6.4 5.2 %collective-permute-start = (f32[32,4,128]{2,1,0:T(4,128)S(1)}, f32[32,4,128]{2,1,0:T(4,128)S(1)}, u32[]{:S(2)}, u32[]{:S(2)}) collective-permute-start(f32[32,4,128]{2,1,0:T(4,128)S(1)} %get-tuple-element.23), channel_id=1, source_target_pairs={{1,0},{2,1},{3,2},{4,3},{5,4},{6,5},{7,6},{0,7},{9,8},{10,9},{11,1... | collective-permute-start | bytes 196616 | tf_op jit(solution)/shard_map/ppermute | solution.py:213
  11.6 1.3 collective-permute-done
  12.9 4.5 %collective-permute-done.1 = f32[32,4,128]{2,1,0:T(4,128)S(1)} collective-permute-done((f32[32,4,128]{2,1,0:T(4,128)S(1)}, f32[32,4,128]{2,1,0:T(4,128)S(1)}, u32[]{:S(2)}, u32[]{:S(2)}) %collective-permute-start.1) | collective-permute-done | bytes 65568 | tf_op jit(solution)/shard_map/ppermute | solution.py:212
  18.0 4.0 %collective-permute-start.3 = (f32[4,136,128]{2,1,0:T(8,128)S(1)}, f32[4,136,128]{2,1,0:T(8,128)S(1)}, u32[]{:S(2)}, u32[]{:S(2)}) collective-permute-start(f32[4,136,128]{2,1,0:T(8,128)S(1)} %get-tuple-element.21), channel_id=1, source_target_pairs={{8,0},{16,8},{24,16},{9,1},{17,9},{25,17},{10,2},{18,10},{26,18},{... | collective-permute-start | bytes 835592 | tf_op jit(solution)/shard_map/ppermute | solution.py:213
  22.0 3.0 %collective-permute-start.2 = (f32[4,136,128]{2,1,0:T(8,128)S(1)}, f32[4,136,128]{2,1,0:T(8,128)S(1)}, u32[]{:S(2)}, u32[]{:S(2)}) collective-permute-start(f32[4,136,128]{2,1,0:T(8,128)S(1)} %get-tuple-element.22), channel_id=1, source_target_pairs={{0,8},{8,16},{16,24},{1,9},{9,17},{17,25},{2,10},{10,18},{18,26},{... | collective-permute-start | bytes 835592 | tf_op jit(solution)/shard_map/ppermute | solution.py:212
  25.9 8.9 %pack.1 = bf16[32,176,128]{2,1,0:T(8,128)(2,1)} custom-call(s32[4096]{0:T(1024)} %slot_ref.1, bf16[80,4096]{1,0:T(8,128)(2,1)} %weights_ref.1, f32[8,4096]{1,0:T(8,128)} %stack.31.extras_ref), custom_call_target="tpu_custom_call" | custom-call | bytes 31457280 | tf_op jit(solution)/shard_map/pack/pallas_call | solution.py:243
  35.6 2.4 %all-to-all-start = ((bf16[32,176,128]{2,1,0:T(8,128)(2,1)}), bf16[32,176,128]{2,1,0:T(8,128)(2,1)S(1)}, u32[]{:S(2)}, u32[]{:S(2)}) async-start(bf16[32,176,128]{2,1,0:T(8,128)(2,1)} %pack.1), calls=%async_computation | async-start | bytes 2883584 | tf_op jit(solution)/shard_map/all_to_all | solution.py:260
  38.0 2.9 %pad_maximum_fusion.field_ref = f32[40,136,128]{2,1,0:T(8,128)} fusion(f32[4,136,128]{2,1,0:T(8,128)} %copy-done.3, f32[32,4,128]{2,1,0:T(4,128)} %copy-done.6, f32[32,4,128]{2,1,0:T(4,128)} %copy-done.5, f32[32,128,128]{2,1,0:T(8,128)S(1)} %bitcast_add_fusion, f32[4,136,128]{2,1,0:T(8,128)} %copy-done.4), kind=kLoop, calls=%fused_computation | loop fusion | flops 2785280 | bytes 5570560 | tf_op jit(solution)/shard_map/concatenate | solution.py:261
  40.9 11.8 %forward.1 = (f32[32,128,128]{2,1,0:T(8,128)}, f32[40,136,128]{2,1,0:T(8,128)}) custom-call(f32[40,136,128]{2,1,0:T(8,128)} %pad_maximum_fusion.field_ref), custom_call_target="tpu_custom_call" | custom-call | flops 27852800 | bytes 8355840 | tf_op jit(solution)/shard_map/forward/pallas_call | solution.py:263
  52.7 20.2 %all-to-all-done.got_ref = bf16[32,176,128]{2,1,0:T(8,128)(2,1)S(1)} async-done(((bf16[32,176,128]{2,1,0:T(8,128)(2,1)}), bf16[32,176,128]{2,1,0:T(8,128)(2,1)S(1)}, u32[]{:S(2)}, u32[]{:S(2)}) %all-to-all-start) | async-done | bytes 1441824 | tf_op jit(solution)/shard_map/all_to_all | solution.py:260
  74.0 5.6 %unpack.1 = (f32[8192,128]{1,0:T(8,128)}, s32[32,256]{1,0:T(8,128)}) custom-call(bf16[32,176,128]{2,1,0:T(8,128)(2,1)} %copy-done.1), custom_call_target="tpu_custom_call" | custom-call | tf_op jit(solution)/shard_map/unpack/pallas_call | solution.py:277
  79.6 1.4 copy.18
  81.0 29.7 %observe.1 = f32[4096,128]{1,0:T(8,128)} custom-call(s32[8192]{0:T(1024)} %bitcast.24, f32[8192,128]{1,0:T(8,128)} %get-tuple-element.14.got_ref, f32[4096,128]{1,0:T(8,128)} %bitcast.23), custom_call_target="tpu_custom_call" | custom-call | tf_op jit(solution)/shard_map/observe/pallas_call | solution.py:288
  110.7 1.9 %convert.10 = bf16[32,128,128]{2,1,0:T(8,128)(2,1)S(1)} convert(f32[32,128,128]{2,1,0:T(8,128)} %bitcast.20) | non-fusion elementwise | flops 524288 | bytes 3145728 | tf_op jit(solution)/shard_map/convert.5
  112.7 2.4 %collective-permute-start.4 = (bf16[32,4,128]{2,1,0:T(4,128)(2,1)S(1)}, bf16[32,4,128]{2,1,0:T(4,128)(2,1)S(1)}, u32[]{:S(2)}, u32[]{:S(2)}) collective-permute-start(bf16[32,4,128]{2,1,0:T(4,128)(2,1)S(1)} %get-tuple-element.25), channel_id=1, source_target_pairs={{1,0},{2,1},{3,2},{4,3},{5,4},{6,5},{7,6},{0,7},{9,8},{10,9},{11,1... | collective-permute-start | bytes 98312 | tf_op jit(solution)/shard_map/ppermute | solution.py:213
  116.2 4.4 %collective-permute-done.5 = bf16[32,4,128]{2,1,0:T(4,128)(2,1)S(1)} collective-permute-done((bf16[32,4,128]{2,1,0:T(4,128)(2,1)S(1)}, bf16[32,4,128]{2,1,0:T(4,128)(2,1)S(1)}, u32[]{:S(2)}, u32[]{:S(2)}) %collective-permute-start.5) | collective-permute-done | bytes 32800 | tf_op jit(solution)/shard_map/ppermute | solution.py:212
  120.6 3.2 %collective-permute-start.6 = (bf16[4,136,128]{2,1,0:T(8,128)(2,1)S(1)}, bf16[4,136,128]{2,1,0:T(8,128)(2,1)S(1)}, u32[]{:S(2)}, u32[]{:S(2)}) collective-permute-start(bf16[4,136,128]{2,1,0:T(8,128)(2,1)S(1)} %get-tuple-element.19), channel_id=1, source_target_pairs={{0,8},{8,16},{16,24},{1,9},{9,17},{17,25},{2,10},{10,18},{18,26},{... | collective-permute-start | bytes 417800 | tf_op jit(solution)/shard_map/ppermute | solution.py:212
  123.8 1.9 %collective-permute-start.7 = (bf16[4,136,128]{2,1,0:T(8,128)(2,1)S(1)}, bf16[4,136,128]{2,1,0:T(8,128)(2,1)S(1)}, u32[]{:S(2)}, u32[]{:S(2)}) collective-permute-start(bf16[4,136,128]{2,1,0:T(8,128)(2,1)S(1)} %get-tuple-element.20), channel_id=1, source_target_pairs={{8,0},{16,8},{24,16},{9,1},{17,9},{25,17},{10,2},{18,10},{26,18},{... | collective-permute-start | bytes 417800 | tf_op jit(solution)/shard_map/ppermute | solution.py:213
  125.8 4.3 %collective-permute-done.7 = bf16[4,136,128]{2,1,0:T(8,128)(2,1)S(1)} collective-permute-done((bf16[4,136,128]{2,1,0:T(8,128)(2,1)S(1)}, bf16[4,136,128]{2,1,0:T(8,128)(2,1)S(1)}, u32[]{:S(2)}, u32[]{:S(2)}) %collective-permute-start.7) | collective-permute-done | bytes 139296 | tf_op jit(solution)/shard_map/ppermute | solution.py:213
  130.2 1.8 %pad_maximum_fusion.1.field_ref = f32[40,136,128]{2,1,0:T(8,128)} fusion(f32[4,136,128]{2,1,0:T(8,128)S(1)} %convert_element_type.39, f32[32,4,128]{2,1,0:T(4,128)S(1)} %convert_element_type.37, f32[32,4,128]{2,1,0:T(4,128)S(1)} %convert_element_type.36, f32[32,128,128]{2,1,0:T(8,128)S(1)} %bitcast.22, f32[4,136,128]{2,1,0:T(8,128)S(1)} %convert_element_type.38), kind=kLoop, calls=%fused_computation.1 | loop fusion | flops 2785280 | bytes 5570560 | tf_op jit(solution)/shard_map/concatenate | solution.py:221
  131.9 9.6 %adjoint.1 = f32[32,128,128]{2,1,0:T(8,128)} custom-call(f32[40,136,128]{2,1,0:T(8,128)} %pad_maximum_fusion.1.field_ref, f32[40,136,128]{2,1,0:T(8,128)} %get-tuple-element.18.kappa_ref), custom_call_target="tpu_custom_call" | custom-call | tf_op jit(solution)/shard_map/adjoint/pallas_call | solution.py:299
  141.6 4.6 %fusion.5 = f32[80,32,128]{2,0,1:T(8,128)S(1)} fusion(f32[32,128,128]{2,1,0:T(8,128)} %adjoint.1, f32[80,32,128]{2,1,0:T(8,128)S(1)} %copy-done.2, f32[80,80]{1,0:T(8,128)S(1)} %copy-done.7), kind=kOutput, calls=%fused_computation.6 | convolution fusion | flops 314900480 | bytes 4744192 | tf_op jit(solution)/shard_map/jk,abj->kab/dot_general | solution.py:308
  146.2 1.5 copy.14
  (43 shorter events, 5.6 us)
Async XLA Ops:
  6.4 18.7 %copy-start.9 = (bf16[4096]{0:T(1024)(128)(2,1)S(1)}, bf16[4096]{0:T(1024)(128)(2,1)}, u32[]{:S(2)}) copy-start(bf16[4096]{0:T(1024)(128)(2,1)} %param.12) | copy-start | bytes 24580
  6.4 18.7 %copy-start.10 = (bf16[4096]{0:T(1024)(128)(2,1)S(1)}, bf16[4096]{0:T(1024)(128)(2,1)}, u32[]{:S(2)}) copy-start(bf16[4096]{0:T(1024)(128)(2,1)} %param.13) | copy-start | bytes 24580
  6.4 18.7 %copy-start.8 = (s32[4096]{0:T(1024)S(1)}, s32[4096]{0:T(1024)}, u32[]{:S(2)}) copy-start(s32[4096]{0:T(1024)} %param.15) | copy-start | bytes 49156
  6.4 6.5 %collective-permute-start = (f32[32,4,128]{2,1,0:T(4,128)S(1)}, f32[32,4,128]{2,1,0:T(4,128)S(1)}, u32[]{:S(2)}, u32[]{:S(2)}) collective-permute-start(f32[32,4,128]{2,1,0:T(4,128)S(1)} %get-tuple-element.23), channel_id=1, source_target_pairs={{1,0},{2,1},{3,2},{4,3},{5,4},{6,5},{7,6},{0,7},{9,8},{10,9},{11,1... | collective-permute-start | bytes 196616 | tf_op jit(solution)/shard_map/ppermute | solution.py:213
  11.6 5.8 %collective-permute-start.1 = (f32[32,4,128]{2,1,0:T(4,128)S(1)}, f32[32,4,128]{2,1,0:T(4,128)S(1)}, u32[]{:S(2)}, u32[]{:S(2)}) collective-permute-start(f32[32,4,128]{2,1,0:T(4,128)S(1)} %get-tuple-element.24), channel_id=1, source_target_pairs={{0,1},{1,2},{2,3},{3,4},{4,5},{5,6},{6,7},{7,0},{8,9},{9,10},{10,1... | collective-permute-start | bytes 196616 | tf_op jit(solution)/shard_map/ppermute | solution.py:212
  12.9 4.5 %copy-start.5 = (f32[32,4,128]{2,1,0:T(4,128)}, f32[32,4,128]{2,1,0:T(4,128)S(1)}, u32[]{:S(2)}) copy-start(f32[32,4,128]{2,1,0:T(4,128)S(1)} %collective-permute-done) | copy-start | bytes 196612
  17.4 0.6 copy-start.6
  18.0 16.8 %collective-permute-start.3 = (f32[4,136,128]{2,1,0:T(8,128)S(1)}, f32[4,136,128]{2,1,0:T(8,128)S(1)}, u32[]{:S(2)}, u32[]{:S(2)}) collective-permute-start(f32[4,136,128]{2,1,0:T(8,128)S(1)} %get-tuple-element.21), channel_id=1, source_target_pairs={{8,0},{16,8},{24,16},{9,1},{17,9},{25,17},{10,2},{18,10},{26,18},{... | collective-permute-start | bytes 835592 | tf_op jit(solution)/shard_map/ppermute | solution.py:213
  22.0 12.8 %collective-permute-start.2 = (f32[4,136,128]{2,1,0:T(8,128)S(1)}, f32[4,136,128]{2,1,0:T(8,128)S(1)}, u32[]{:S(2)}, u32[]{:S(2)}) collective-permute-start(f32[4,136,128]{2,1,0:T(8,128)S(1)} %get-tuple-element.22), channel_id=1, source_target_pairs={{0,8},{8,16},{16,24},{1,9},{9,17},{17,25},{2,10},{10,18},{18,26},{... | collective-permute-start | bytes 835592 | tf_op jit(solution)/shard_map/ppermute | solution.py:212
  34.8 0.7 copy-start.3
  34.8 0.8 copy-start.4
  35.6 37.3 %all-to-all-start = ((bf16[32,176,128]{2,1,0:T(8,128)(2,1)}), bf16[32,176,128]{2,1,0:T(8,128)(2,1)S(1)}, u32[]{:S(2)}, u32[]{:S(2)}) async-start(bf16[32,176,128]{2,1,0:T(8,128)(2,1)} %pack.1), calls=%async_computation | async-start | bytes 2883584 | tf_op jit(solution)/shard_map/all_to_all | solution.py:260
  72.9 1.1 copy-start.1
  110.7 9.8 %copy-start = (f32[4096,128]{1,0:T(8,128)S(1)}, f32[4096,128]{1,0:T(8,128)}, u32[]{:S(2)}) copy-start(f32[4096,128]{1,0:T(8,128)} %observe.1) | copy-start | bytes 6291460
  112.7 3.5 %collective-permute-start.4 = (bf16[32,4,128]{2,1,0:T(4,128)(2,1)S(1)}, bf16[32,4,128]{2,1,0:T(4,128)(2,1)S(1)}, u32[]{:S(2)}, u32[]{:S(2)}) collective-permute-start(bf16[32,4,128]{2,1,0:T(4,128)(2,1)S(1)} %get-tuple-element.25), channel_id=1, source_target_pairs={{1,0},{2,1},{3,2},{4,3},{5,4},{6,5},{7,6},{0,7},{9,8},{10,9},{11,1... | collective-permute-start | bytes 98312 | tf_op jit(solution)/shard_map/ppermute | solution.py:213
  115.0 5.5 %collective-permute-start.5 = (bf16[32,4,128]{2,1,0:T(4,128)(2,1)S(1)}, bf16[32,4,128]{2,1,0:T(4,128)(2,1)S(1)}, u32[]{:S(2)}, u32[]{:S(2)}) collective-permute-start(bf16[32,4,128]{2,1,0:T(4,128)(2,1)S(1)} %get-tuple-element.26), channel_id=1, source_target_pairs={{0,1},{1,2},{2,3},{3,4},{4,5},{5,6},{6,7},{7,0},{8,9},{9,10},{10,1... | collective-permute-start | bytes 98312 | tf_op jit(solution)/shard_map/ppermute | solution.py:212
  120.6 5.2 %collective-permute-start.6 = (bf16[4,136,128]{2,1,0:T(8,128)(2,1)S(1)}, bf16[4,136,128]{2,1,0:T(8,128)(2,1)S(1)}, u32[]{:S(2)}, u32[]{:S(2)}) collective-permute-start(bf16[4,136,128]{2,1,0:T(8,128)(2,1)S(1)} %get-tuple-element.19), channel_id=1, source_target_pairs={{0,8},{8,16},{16,24},{1,9},{9,17},{17,25},{2,10},{10,18},{18,26},{... | collective-permute-start | bytes 417800 | tf_op jit(solution)/shard_map/ppermute | solution.py:212
  123.8 6.4 %collective-permute-start.7 = (bf16[4,136,128]{2,1,0:T(8,128)(2,1)S(1)}, bf16[4,136,128]{2,1,0:T(8,128)(2,1)S(1)}, u32[]{:S(2)}, u32[]{:S(2)}) collective-permute-start(bf16[4,136,128]{2,1,0:T(8,128)(2,1)S(1)} %get-tuple-element.20), channel_id=1, source_target_pairs={{8,0},{16,8},{24,16},{9,1},{17,9},{25,17},{10,2},{18,10},{26,18},{... | collective-permute-start | bytes 417800 | tf_op jit(solution)/shard_map/ppermute | solution.py:213
  131.9 9.6 %copy-start.2 = (f32[80,32,128]{2,1,0:T(8,128)S(1)}, f32[80,32,128]{2,1,0:T(8,128)}, u32[]{:S(2)}) copy-start(f32[80,32,128]{2,1,0:T(8,128)} %param.8) | copy-start | bytes 3932164
  131.9 9.6 %copy-start.7 = (f32[80,80]{1,0:T(8,128)S(1)}, f32[80,80]{1,0:T(8,128)}, u32[]{:S(2)}) copy-start(f32[80,80]{1,0:T(8,128)} %param.9) | copy-start | bytes 76804
